TPU v7x, 128 devices: a whole 4x4x4 slice. The times are simulated.
128 devices in a mesh: expert: 4 (over z_hi, core), context: 16 (over y, x), dp: 2 (over z_lo).
Axes of the slice: x: 4, y: 4, z: 4 (z_hi: 2, z_lo: 2; z = z_hi * 2 + z_lo), core: 2. Of those that a mesh axis runs over, the one named last changes fastest.
Arguments:
- inputs: bfloat16 [8, 2048, 768], P(('expert', 'dp'), 'context'), may hold values from -6 to 6
- cotangent: bfloat16 [8, 2048, 768], P(('expert', 'dp'), 'context'), may hold values from -6 to 6
- norm1_gain: bfloat16 [768], replicated, may hold values from 0.5 to 1.5
- w_query: bfloat16 [768, 768], replicated, may hold values from -0.21875 to 0.21875
- w_key: bfloat16 [768, 768], replicated, may hold values from -0.21875 to 0.21875
- w_value: bfloat16 [768, 768], replicated, may hold values from -0.21875 to 0.21875
- w_output: bfloat16 [768, 768], replicated, may hold values from -3.5 to 3.5
- bias_table: bfloat16 [32, 12], replicated, may hold values from -4 to 4
- buckets: int32 [4095], replicated, may hold values from 0 to 31
- norm2_gain: bfloat16 [768], replicated, may hold values from 0.5 to 1.5
- w_router: bfloat16 [768, 4], replicated, may hold values from -0.15625 to 0.15625
- routes: int32 [8, 2048, 1], P(('expert', 'dp'), 'context'), may hold values from 0 to 3; in each aligned block of 128 rows (0 to 127, 128 to 255, ..., all dimensions but the last counted through in order) at most 40 rows name the same one
- w_in: bfloat16 [4, 768, 3072], P('expert'), may hold values from -0.21875 to 0.21875
- w_out: bfloat16 [4, 3072, 768], P('expert'), may hold values from -0.4375 to 0.4375
Outputs:
- mixed: bfloat16 [8, 2048, 768], P(('expert', 'dp'), 'context')
- grad_input: bfloat16 [8, 2048, 768], P(('expert', 'dp'), 'context')
- grad_norm1_gain: float32 [768], replicated
- grad_w_query: float32 [768, 768], replicated
- grad_w_key: float32 [768, 768], replicated
- grad_w_value: float32 [768, 768], replicated
- grad_w_output: float32 [768, 768], replicated
- grad_bias_table: float32 [32, 12], replicated
- grad_norm2_gain: float32 [768], replicated
- grad_w_router: float32 [768, 4], replicated
- grad_w_in: float32 [4, 768, 3072], P('expert', None, ('context', 'dp'))
- grad_w_out: float32 [4, 3072, 768], P('expert', ('context', 'dp'))
Inputs may be any that keep to these rules, and one draw needn't show every extreme that they name: `routes`: among the 128 rows of one device (aligned blocks of the flattened sequences), no expert is named more than 40 times, and in every draw some expert is named exactly 40 times in some device's rows.
All inputs are finite; a program needn't handle non-finite values.
Results may differ from a plain program's by a relative error of at most 0.025.
Values may be sent and summed in bfloat16 or wider, within the bound.
No kernel may reach another device: no remote copies, remote signals or barrier semaphores. Data moves between devices by JAX's collectives and lax.ppermute only.
A program may use at most 384 MiB of HBM per device.

v0:
```python
import functools
import math

import jax
import jax.numpy as jnp
from jax import lax
from jax.experimental import pallas as pl
from jax.experimental.pallas import tpu as pltpu
from jax.sharding import PartitionSpec as P

EPS = 1e-06
F32 = jnp.float32
BF16 = jnp.bfloat16
NN = (((1,), (0,)), ((), ()))
NT = (((1,), (1,)), ((), ()))
HIGHEST = lax.Precision.HIGHEST
MIB = 1 << 20


def mm(left, right, dims=NN):
    return lax.dot_general(left, right, dims, preferred_element_type=F32)


def rms_stats(values):
    return lax.rsqrt(jnp.mean(values * values, axis=-1, keepdims=True) + EPS)


def rms_back(grad, values, scale, gain):
    weighted = grad * gain
    inner = jnp.mean(weighted * values, axis=-1, keepdims=True)
    return scale * weighted - values * (scale * scale * scale * inner)


def gelu_parts(u):
    c = math.sqrt(2.0 / math.pi)
    sq = u * u
    t = jnp.tanh(c * u * (1.0 + 0.044715 * sq))
    half = 0.5 * (1.0 + t)
    slope = half + (0.5 * c) * u * (1.0 - t * t) * (1.0 + (3 * 0.044715) * sq)
    return u * half, slope


def first_half(shape, size):
    return lax.broadcasted_iota(jnp.int32, shape, 1) < size


def split_pair(pair, size):
    first = first_half(pair.shape, size)
    zero = jnp.zeros_like(pair)
    return jnp.concatenate([jnp.where(first, pair, zero), jnp.where(first, zero, pair)], 0)


def join_pair(stacked, size):
    rows = stacked.shape[0] // 2
    return jnp.where(first_half((rows, 2 * size), size), stacked[:rows], stacked[rows:])


def attend_kernel(act_ref, own_ref, wq_ref, wk_ref, wv_ref, win_ref, *refs):
    q_ref, k_ref, v_ref, o_ref, inv_ref, p_ref, s_ref, m_ref, ext_ref = refs[-9:]
    tok = own_ref.shape[0]
    length = act_ref.shape[0]
    wide = win_ref.shape[2]
    lanes = wq_ref.shape[1]
    size = lanes // 2
    query = mm(own_ref[...], wq_ref[...]).astype(BF16)
    query = query.astype(F32) * (1.0 / math.sqrt(size))
    q_ref[...] = query.astype(BF16)
    both = mm(act_ref[...], jnp.concatenate([wk_ref[...], wv_ref[...]], 1)).astype(BF16)
    k_ref[...] = both[:, :lanes]
    v_ref[...] = both[:, lanes:]
    ext_ref[:, :lanes] = both[:, lanes:]
    ext_ref[:, lanes:] = jnp.ones((length, lanes), BF16)
    s_ref[...] = mm(split_pair(query, size).astype(BF16), k_ref[...], NT)
    sub = lax.broadcasted_iota(jnp.int32, (16, wide), 0)

    def first_band(head):
        band = jnp.broadcast_to(win_ref[0, head : head + 1, :], (16, wide))
        band = pltpu.roll(band, wide - (tok - 1), 1)
        for bit in (1, 2, 4, 8):
            band = jnp.where((sub & bit) != 0, pltpu.roll(band, bit, 1), band)
        return band

    def rows_of(head, r):
        return pl.ds(pl.multiple_of(head * tok + r * 16, 16), 16)

    def add_bias(r, bands):
        for head in range(2):
            rows = rows_of(head, r)
            s = s_ref[rows, :] + bands[head][:, :length]
            s_ref[rows, :] = s
            m_ref[rows, :] = jnp.broadcast_to(jnp.max(s, axis=1, keepdims=True), (16, lanes))
        return tuple(pltpu.roll(band, 16, 1) for band in bands)

    def exponents(r, carry):
        for head in range(2):
            rows = rows_of(head, r)
            top = jnp.concatenate([m_ref[rows, :]] * (length // lanes), 1)
            p_ref[0, rows, :] = jnp.exp(s_ref[rows, :] - top).astype(BF16)
        return carry

    lax.fori_loop(0, tok // 16, add_bias, (first_band(0), first_band(1)))
    lax.fori_loop(0, tok // 16, exponents, 0)
    summed = mm(p_ref[0], ext_ref[...])
    inverse = 1.0 / join_pair(summed[:, lanes:], size)
    inv_ref[...] = inverse
    o_ref[...] = join_pair(summed[:, :lanes], size) * inverse


def attend(act_all, act, w_query, w_key, w_value, window, ready):
    length, width = act_all.shape
    tok = act.shape[0]
    pairs, _, wide = window.shape
    lanes = width // pairs
    column = lambda rows: pl.BlockSpec((rows, lanes), lambda p: (0, p))
    whole = lambda rows: pl.BlockSpec((rows, width), lambda p: (0, 0))
    return pl.pallas_call(
        attend_kernel,
        grid=(pairs,),
        in_specs=[
            whole(length), whole(tok), column(width), column(width), column(width),
            pl.BlockSpec((1, 2, wide), lambda p: (p, 0, 0)),
        ] + [pl.BlockSpec(memory_space=pl.ANY)] * len(ready),
        out_specs=[
            column(tok), column(length), column(length), column(tok), column(tok),
            pl.BlockSpec((1, 2 * tok, length), lambda p: (p, 0, 0)),
        ],
        out_shape=[
            jax.ShapeDtypeStruct((tok, width), BF16),
            jax.ShapeDtypeStruct((length, width), BF16),
            jax.ShapeDtypeStruct((length, width), BF16),
            jax.ShapeDtypeStruct((tok, width), F32),
            jax.ShapeDtypeStruct((tok, width), F32),
            jax.ShapeDtypeStruct((pairs, 2 * tok, length), BF16),
        ],
        scratch_shapes=[
            pltpu.VMEM((2 * tok, length), F32),
            pltpu.VMEM((2 * tok, lanes), F32),
            pltpu.VMEM((length, 2 * lanes), BF16),
        ],
        compiler_params=pltpu.CompilerParams(vmem_limit_bytes=56 * MIB),
        cost_estimate=pl.CostEstimate(
            flops=4 * length * width * width + 8 * tok * length * width,
            bytes_accessed=12 * length * width + 4 * pairs * tok * length,
            transcendentals=2 * pairs * tok * length,
        ),
        name="attend",
    )(act_all, act, w_query, w_key, w_value, window, *ready)


def attend_back_kernel(half_ref, p_ref, do_ref, o_ref, q_ref, k_ref, v_ref, act_ref, own_ref,
                       wqt_ref, wkt_ref, wvt_ref, ready_ref,
                       dq_ref, dkv_ref, grad_ref, gain_ref, diag_ref,
                       dp_ref, ds_ref, delta_ref):
    tok = do_ref.shape[0]
    length = act_ref.shape[0]
    lanes = q_ref.shape[1]
    wide = diag_ref.shape[2]
    size = lanes // 2
    pair = pl.program_id(0)
    grad = do_ref[...].astype(F32)
    grads = split_pair(grad, size)
    delta = jnp.sum(split_pair(grad * o_ref[...], size), axis=1, keepdims=True)
    delta_ref[...] = jnp.broadcast_to(delta, delta_ref.shape)
    dp_ref[...] = mm(grads.astype(BF16), v_ref[...], NT)

    def step(r, totals):
        after = []
        for head in range(2):
            rows = pl.ds(pl.multiple_of(head * tok + r * 16, 16), 16)
            less = jnp.concatenate([delta_ref[rows, :]] * (length // lanes), 1)
            d = p_ref[0, rows, :].astype(F32) * (dp_ref[rows, :] - less)
            ds_ref[rows, :] = d.astype(BF16)
            d = jnp.concatenate([d, jnp.zeros((16, wide - length), F32)], 1)
            after.append(pltpu.roll(totals[head], 16, 1) + d)
        return tuple(after)

    empty = jnp.zeros((16, wide), F32)
    totals = lax.fori_loop(0, tok // 16, step, (empty, empty))
    sub = lax.broadcasted_iota(jnp.int32, (16, wide), 0)
    for head in range(2):
        total = totals[head]
        for bit in (1, 2, 4, 8):
            total = jnp.where((sub & bit) == 0, pltpu.roll(total, bit, 1), total)
        diag_ref[0, head : head + 1, :] = jnp.sum(total, axis=0, keepdims=True)
    dq = join_pair(mm(ds_ref[...], k_ref[...]), size) * (1.0 / math.sqrt(size))
    dq_ref[...] = dq.astype(BF16)
    queries = split_pair(q_ref[...].astype(F32), size)
    dk = mm(queries.T.astype(BF16), ds_ref[...]).astype(BF16)
    dv = mm(grads.T.astype(BF16), p_ref[0]).astype(BF16)
    dkv_ref[0] = dk
    dkv_ref[1] = dv
    weights = mm(jnp.concatenate([dk, dv], 0), act_ref[...])
    parts = (mm(dq.T.astype(BF16), own_ref[...]), weights[:lanes], weights[lanes:])
    gain = jnp.zeros((1, act_ref.shape[1]), F32)
    for i, (found, turned) in enumerate(zip(parts, (wqt_ref, wkt_ref, wvt_ref))):
        grad_ref[i] = found.T.astype(BF16)
        gain = gain + jnp.sum(found * turned[...].astype(F32), axis=0, keepdims=True)

    @pl.when(pair == 0)
    def _():
        gain_ref[...] = gain

    @pl.when(pair > 0)
    def _():
        gain_ref[...] += gain


def attend_back(half, probs, grad_heads, heads, query, key, value, act_all, act, turned, ready):
    length, width = act_all.shape
    tok = query.shape[0]
    pairs = probs.shape[0] // 2
    wide = length + tok
    lanes = width // (2 * pairs)
    column = lambda rows: pl.BlockSpec((rows, lanes), lambda p, h: (0, p + h[0] * pairs))
    whole = lambda rows, cols: pl.BlockSpec((rows, cols), lambda p, h: (0, 0))
    row = pl.BlockSpec((lanes, width), lambda p, h: (p + h[0] * pairs, 0))
    return pl.pallas_call(
        attend_back_kernel,
        grid_spec=pltpu.PrefetchScalarGridSpec(
            num_scalar_prefetch=1,
            grid=(pairs,),
            in_specs=[
                pl.BlockSpec((1, 2 * tok, length), lambda p, h: (p + h[0] * pairs, 0, 0)),
                column(tok), column(tok), column(tok), column(length), column(length),
                whole(length, width), whole(tok, width),
                row, row, row, pl.BlockSpec(memory_space=pl.ANY),
            ],
            out_specs=[
                pl.BlockSpec((tok, lanes), lambda p, h: (0, p)),
                pl.BlockSpec((2, lanes, length), lambda p, h: (0, p, 0)),
                pl.BlockSpec((3, width, lanes), lambda p, h: (0, 0, p)),
                pl.BlockSpec((1, width), lambda p, h: (0, 0)),
                pl.BlockSpec((1, 2, wide), lambda p, h: (p, 0, 0)),
            ],
            scratch_shapes=[
                pltpu.VMEM((2 * tok, length), F32),
                pltpu.VMEM((2 * tok, length), BF16),
                pltpu.VMEM((2 * tok, lanes), F32),
            ],
        ),
        out_shape=[
            jax.ShapeDtypeStruct((tok, width // 2), BF16),
            jax.ShapeDtypeStruct((2, width // 2, length), BF16),
            jax.ShapeDtypeStruct((3, width, width // 2), BF16),
            jax.ShapeDtypeStruct((1, width), F32),
            jax.ShapeDtypeStruct((pairs, 2, wide), F32),
        ],
        compiler_params=pltpu.CompilerParams(vmem_limit_bytes=56 * MIB),
        cost_estimate=pl.CostEstimate(
            flops=4 * length * width * width + 8 * tok * length * width,
            bytes_accessed=8 * length * width + 2 * pairs * tok * length,
            transcendentals=0,
        ),
        name="attend_back",
    )(half, probs, grad_heads, heads, query, key, value, act_all, act, *turned, ready)


def spread_kernel(half_ref, wka_ref, wva_ref, a_ref, wkb_ref, wvb_ref, b_ref, out_ref):
    tok = out_ref.shape[2]
    found = mm(jnp.concatenate([wka_ref[...], wva_ref[...]], 1), jnp.concatenate([a_ref[0], a_ref[1]], 0))
    found += mm(jnp.concatenate([wkb_ref[...], wvb_ref[...]], 1), jnp.concatenate([b_ref[0], b_ref[1]], 0))
    found = found.astype(BF16)
    for i in range(out_ref.shape[0]):
        out_ref[i] = found[:, i * tok : (i + 1) * tok]


def spread(half, w_key, w_value, terms_a, terms_b, tok):
    width = w_key.shape[0]
    length = terms_a.shape[2]
    cols = width // 2
    weight_a = pl.BlockSpec((width, cols), lambda c, h: (0, h[0]))
    weight_b = pl.BlockSpec((width, cols), lambda c, h: (0, 1 - h[0]))
    terms = pl.BlockSpec((2, cols, 2 * tok), lambda c, h: (0, 0, c))
    return pl.pallas_call(
        spread_kernel,
        grid_spec=pltpu.PrefetchScalarGridSpec(
            num_scalar_prefetch=1,
            grid=(length // (2 * tok),),
            in_specs=[weight_a, weight_a, terms, weight_b, weight_b, terms],
            out_specs=pl.BlockSpec((2, width, tok), lambda c, h: (c, 0, 0)),
        ),
        out_shape=jax.ShapeDtypeStruct((length // tok, width, tok), BF16),
        compiler_params=pltpu.CompilerParams(vmem_limit_bytes=56 * MIB),
        cost_estimate=pl.CostEstimate(
            flops=4 * length * width * width, bytes_accessed=6 * length * width, transcendentals=0
        ),
        name="spread",
    )(half, w_key, w_value, terms_a, w_key, w_value, terms_b)


def merge_kernel(mine_ref, other_ref, mine_out_ref, other_out_ref, small_ref, out_ref):
    count = out_ref.shape[0]
    rows = mine_ref.shape[1] // count
    for c in range(count):
        here = slice(c * rows, (c + 1) * rows)
        for i in range(3):
            found = mine_ref[i, here, :].astype(F32) + other_ref[i, here, :].astype(F32)
            out_ref[c, i * rows : (i + 1) * rows, :] = found.astype(BF16)
        found = mine_out_ref[here, :].astype(F32) + other_out_ref[here, :].astype(F32)
        out_ref[c, 3 * rows : 4 * rows, :] = found.astype(BF16)
        out_ref[c, 4 * rows :, :] = small_ref[c]


def merge_halves(mine, other, mine_out, other_out, small):
    count, extra, cols = small.shape
    width = mine.shape[1]
    rows = width // count
    steps = 4
    each = count // steps
    triple = pl.BlockSpec((3, each * rows, cols), lambda c: (0, c, 0))
    single = pl.BlockSpec((each * rows, cols), lambda c: (c, 0))
    return pl.pallas_call(
        merge_kernel,
        grid=(steps,),
        in_specs=[triple, triple, single, single, pl.BlockSpec((each, extra, cols), lambda c: (c, 0, 0))],
        out_specs=pl.BlockSpec((each, 4 * rows + extra, cols), lambda c: (c, 0, 0)),
        out_shape=jax.ShapeDtypeStruct((count, 4 * rows + extra, cols), BF16),
        compiler_params=pltpu.CompilerParams(vmem_limit_bytes=56 * MIB),
        name="merge_halves",
    )(mine, other, mine_out, other_out, small)


def unpack_kernel(core_ref, mine_ref, other_ref, *out_refs):
    count = mine_ref.shape[0]
    rows, width = out_refs[0].shape
    rows = rows // count
    cols = width // 2
    low = core_ref[0] == 0
    for c in range(count):
        for i, out_ref in enumerate(out_refs):
            mine = mine_ref[c, i * rows : (i + 1) * rows, :].astype(F32)
            other = other_ref[c, i * rows : (i + 1) * rows, :].astype(F32)
            out_ref[c * rows : (c + 1) * rows, :cols] = jnp.where(low, mine, other)
            out_ref[c * rows : (c + 1) * rows, cols:] = jnp.where(low, other, mine)


def unpack_halves(core, mine, other):
    count, total, cols = mine.shape
    width = 2 * cols
    rows = width // count
    steps = 4
    each = count // steps
    block = pl.BlockSpec((each, total, cols), lambda c, core: (c, 0, 0))
    return pl.pallas_call(
        unpack_kernel,
        grid_spec=pltpu.PrefetchScalarGridSpec(
            num_scalar_prefetch=1,
            grid=(steps,),
            in_specs=[block, block],
            out_specs=[pl.BlockSpec((each * rows, width), lambda c, core: (c, 0))] * 4,
        ),
        out_shape=[jax.ShapeDtypeStruct((width, width), F32)] * 4,
        compiler_params=pltpu.CompilerParams(vmem_limit_bytes=56 * MIB),
        name="unpack_halves",
    )(core, mine, other)


def expert_kernel(rows_ref, win_ref, wout_ref, out_ref, total_ref):
    width = win_ref.shape[0]
    step = pl.program_id(0)
    sent = rows_ref[:, :width]
    grad = rows_ref[:, width:]
    hidden, slope = gelu_parts(mm(sent, win_ref[...]))
    grad_pre = (mm(grad, wout_ref[...], NT) * slope).astype(BF16)
    forward = mm(hidden.astype(BF16), wout_ref[...])
    backward = mm(grad_pre, win_ref[...], NT)

    @pl.when(step == 0)
    def _():
        total_ref[:, :width] = forward
        total_ref[:, width:] = backward

    @pl.when(step > 0)
    def _():
        total_ref[:, :width] += forward
        total_ref[:, width:] += backward

    @pl.when(step == pl.num_programs(0) - 1)
    def _():
        out_ref[...] = total_ref[...].astype(BF16)


def expert_both(rows, w_in, w_out):
    count, double = rows.shape
    width, units = w_in.shape
    chunk = 768 if units % 768 == 0 else units
    return pl.pallas_call(
        expert_kernel,
        grid=(units // chunk,),
        in_specs=[
            pl.BlockSpec((count, double), lambda c: (0, 0)),
            pl.BlockSpec((width, chunk), lambda c: (0, c)),
            pl.BlockSpec((chunk, width), lambda c: (c, 0)),
        ],
        out_specs=pl.BlockSpec((count, double), lambda c: (0, 0)),
        out_shape=jax.ShapeDtypeStruct((count, double), BF16),
        scratch_shapes=[pltpu.VMEM((count, double), F32)],
        compiler_params=pltpu.CompilerParams(vmem_limit_bytes=56 * MIB),
        cost_estimate=pl.CostEstimate(
            flops=8 * count * width * units, bytes_accessed=4 * width * units, transcendentals=count * units
        ),
        name="expert_both",
    )(rows, w_in, w_out)


def expert_grad_kernel(place_ref, *refs):
    row_refs, (wint_ref, wout_ref, out_ref) = refs[:-3], refs[-3:]
    width = wint_ref.shape[1]
    rows = jnp.concatenate([ref[...] for ref in row_refs], 0)
    sent = rows[:, :width]
    grad = rows[:, width:]
    hidden, slope = gelu_parts(mm(wint_ref[...], sent, NT))
    grad_pre = (mm(wout_ref[...], grad, NT) * slope).astype(BF16)
    found = (mm(grad_pre, sent).astype(BF16), mm(hidden.astype(BF16), grad).astype(BF16))
    share = out_ref.shape[3]
    for d in range(2):
        to = lax.rem(d + place_ref[1], 2)
        for i in range(2):
            out_ref[0, to, i] = found[i][d * share : (d + 1) * share]


def expert_grads(place, parts, w_in_t, w_out, side):
    units, width = w_out.shape
    count = sum(part.shape[0] for part in parts)
    chunk = units // side
    weight = pl.BlockSpec((chunk, width), lambda c, place: (c, 0))
    return pl.pallas_call(
        expert_grad_kernel,
        grid_spec=pltpu.PrefetchScalarGridSpec(
            num_scalar_prefetch=1,
            grid=(side,),
            in_specs=[pl.BlockSpec(part.shape, lambda c, place: (0, 0)) for part in parts] + [weight, weight],
            out_specs=pl.BlockSpec(
                (1, 2, 2, chunk // 2, width),
                lambda c, place: (lax.rem(c + side - place[0], side), 0, 0, 0, 0),
            ),
        ),
        out_shape=jax.ShapeDtypeStruct((side, 2, 2, chunk // 2, width), BF16),
        compiler_params=pltpu.CompilerParams(vmem_limit_bytes=56 * MIB),
        cost_estimate=pl.CostEstimate(
            flops=8 * count * width * units, bytes_accessed=8 * width * units, transcendentals=count * units
        ),
        name="expert_grads",
    )(place, *parts, w_in_t, w_out)


def per_device(
    ctx_count,
    dp_count,
    inputs,
    cotangent,
    norm1_gain,
    w_query,
    w_key,
    w_value,
    w_output,
    bias_table,
    buckets,
    norm2_gain,
    w_router,
    routes,
    w_in,
    w_out,
):
    tok_count, width = inputs.shape[1:]
    length = (buckets.shape[0] + 1) // 2
    bucket_count, head_count = bias_table.shape
    expert_count = w_router.shape[1]
    capacity = (tok_count * 5 + 4 * expert_count - 1) // (4 * expert_count)
    side = math.isqrt(ctx_count)
    units = w_in.shape[2]
    context = lax.axis_index("context")
    ctx_y, ctx_x = context // side, context % side
    dp = lax.axis_index("dp")

    def ring(values, along_y, step):
        pairs = []
        for c in range(ctx_count):
            y, x = divmod(c, side)
            to = ((y + step) % side) * side + x if along_y else y * side + (x + step) % side
            pairs.append((c, to))
        return lax.ppermute(values, "context", pairs)

    inputs_f = inputs[0].astype(F32)
    gain1 = norm1_gain.astype(F32)
    scale1 = rms_stats(inputs_f)
    act = (inputs_f * scale1 * gain1).astype(BF16)
    act_all = lax.all_gather(act, "context", axis=0, tiled=True)

    padded = jnp.pad(buckets, (0, 1))
    start = length - tok_count - context * tok_count
    near = lax.dynamic_slice_in_dim(padded, start, length + tok_count)
    onehot = (jnp.arange(bucket_count, dtype=jnp.int32)[:, None] == near[None, :]).astype(BF16)
    window = lax.dot_general(bias_table, onehot, (((0,), (0,)), ((), ())), preferred_element_type=F32)
    window = window.reshape(head_count // 2, 2, length + tok_count)

    route = routes[0, :, 0]
    chosen = (route[:, None] == jnp.arange(expert_count, dtype=jnp.int32)[None, :]).astype(jnp.int32)
    chosen_f = chosen.astype(F32)
    slot_of = jnp.sum((jnp.cumsum(chosen, axis=0) - 1) * chosen, axis=-1)
    target = route * capacity + slot_of
    slots = jnp.arange(expert_count * capacity, dtype=jnp.int32)
    dispatch = (slots[:, None] == target[None, :]).astype(BF16)
    collect = (target[:, None] == slots[None, :]).astype(BF16)
    quarter = units // side
    w_in_slice = lax.dynamic_slice_in_dim(w_in[0], ctx_y * quarter, quarter, 1).T
    w_out_slice = lax.dynamic_slice_in_dim(w_out[0], ctx_y * quarter, quarter, 0)

    turned = (w_query.T, w_key.T, w_value.T)
    ready = (w_in_slice, w_out_slice) + turned
    query, key, value, heads_f, inverse, probs = attend(
        act_all, act, w_query, w_key, w_value, window, ready
    )
    heads_out = heads_f.astype(BF16)
    resid = inputs_f + mm(heads_out, w_output)
    gain2 = norm2_gain.astype(F32)
    scale2 = rms_stats(resid)
    normed2 = resid * scale2 * gain2
    router = w_router.astype(F32)
    logits = jnp.dot(normed2, router, precision=HIGHEST)
    router_exp = jnp.exp(logits - jnp.max(logits, axis=-1, keepdims=True))
    router_probs = router_exp / jnp.sum(router_exp, axis=-1, keepdims=True)
    gate = jnp.sum(router_probs * chosen_f, axis=-1)
    grad_out = cotangent[0].astype(F32)
    grad_picked = gate[:, None] * grad_out
    going = jnp.concatenate([normed2.astype(BF16), grad_picked.astype(BF16)], 1)
    going = mm(dispatch, going).astype(BF16).reshape(expert_count, capacity, 2 * width)
    arrived = lax.all_to_all(going, "expert", split_axis=0, concat_axis=0, tiled=True)
    arrived = arrived.reshape(expert_count * capacity, 2 * width)
    results = expert_both(arrived, w_in[0], w_out[0])
    results = results.reshape(expert_count, capacity, 2 * width)
    returned = lax.all_to_all(results, "expert", split_axis=0, concat_axis=0, tiled=True)
    returned = mm(collect, returned.reshape(expert_count * capacity, 2 * width))
    picked, grad_sent = returned[:, :width], returned[:, width:]
    mixed = resid + gate[:, None] * picked

    parts = [arrived] + [ring(arrived, True, step) for step in range(1, side)]
    shares = expert_grads(jnp.stack([ctx_x, dp]).astype(jnp.int32), parts, w_in_slice, w_out_slice, side)
    expert_sum = shares[0, 0].astype(F32)
    for step in range(side):
        for flip in range(2):
            if step == 0 and flip == 0:
                continue
            route_pairs = []
            for c in range(ctx_count):
                to = c // side * side + (c % side + step) % side
                for d in range(2):
                    route_pairs.append((c * 2 + d, to * 2 + (d ^ flip)))
            moved = lax.ppermute(shares[step, flip], ("context", "dp"), route_pairs)
            expert_sum = expert_sum + moved.astype(F32)
    grad_w_in_out = expert_sum[0].T[None]
    grad_w_out_out = expert_sum[1][None]

    grad_gate = jnp.sum(grad_out * picked, axis=-1)
    grad_logits = (grad_gate * gate)[:, None] * (chosen_f - router_probs)
    grad_router = lax.dot_general(grad_logits, normed2, (((0,), (0,)), ((), ())), precision=HIGHEST)
    grad_normed2 = grad_sent + jnp.dot(grad_logits, router.T, precision=HIGHEST)
    grad_gain2 = jnp.sum(grad_normed2 * resid * scale2, axis=0)
    grad_resid = rms_back(grad_normed2, resid, scale2, gain2) + grad_out
    grad_attn = grad_resid.astype(BF16)
    grad_heads = mm(grad_attn, w_output, NT).astype(BF16)
    scaled = (grad_heads.astype(F32) * inverse).astype(BF16)

    expert = lax.axis_index("expert")
    core = (expert % 2)[None]
    swap = [(e, e ^ 1) for e in range(expert_count)]
    cols = width // 2
    both_out = []
    for half in (1 - core[0], core[0]):
        attn_half = lax.dynamic_slice_in_dim(grad_attn, half * cols, cols, 1)
        both_out.append(jnp.dot(heads_out.T, attn_half, preferred_element_type=F32).astype(BF16))
    other_out = lax.ppermute(both_out[0], "expert", swap)
    back = functools.partial(
        attend_back, probs=probs, grad_heads=scaled, heads=heads_f, query=query, key=key, value=value,
        act_all=act_all, act=act, turned=turned,
    )
    dq_a, terms_a, grads_a, gain_a, diag_a = back(1 - core, ready=arrived)
    other = lax.ppermute(grads_a, "expert", swap)
    dq_b, terms_b, grads_b, gain_b, diag_b = back(core, ready=shares)
    part = spread(core, w_key, w_value, terms_b, terms_a, tok_count)
    low = core[0] == 0
    in_order = lambda a, b, axis: jnp.concatenate([jnp.where(low, b, a), jnp.where(low, a, b)], axis)
    diagonals = in_order(diag_a, diag_b, 0)
    diagonals = diagonals.reshape(head_count, length + tok_count)
    grad_table = lax.dot_general(
        diagonals, onehot.astype(F32), (((1,), (1,)), ((), ())), precision=HIGHEST
    )
    small = jnp.concatenate(
        [(gain_a + gain_b)[0] / gain1, grad_gain2, grad_router.reshape(-1), grad_table.reshape(-1)]
    )
    small = jnp.pad(small, (0, ctx_count * 16 * cols - small.size)).astype(BF16)
    merged = merge_halves(grads_b, other, both_out[1], other_out, small.reshape(ctx_count, 16, cols))
    merged = lax.all_to_all(merged, "context", split_axis=0, concat_axis=0, tiled=True)
    merged = jnp.sum(merged.astype(F32), axis=0).astype(BF16)
    part, merged = lax.optimization_barrier((part, merged))
    total = merged.astype(F32)
    depth = expert_count // 2 * dp_count
    for step in range(1, depth):
        pairs = []
        for e in range(expert_count):
            for d in range(dp_count):
                z = (e // 2 * dp_count + d + step) % depth
                to = (z // dp_count * 2 + e % 2) * dp_count + z % dp_count
                pairs.append((e * dp_count + d, to))
        total = total + lax.ppermute(merged, ("expert", "dp"), pairs).astype(F32)
    whole = lax.all_gather(total.astype(BF16), "context", axis=0)
    other = lax.ppermute(whole, "expert", swap)
    grad_w_query, grad_w_key, grad_w_value, grad_w_output = unpack_halves(core, whole, other)
    rows = 4 * width // ctx_count
    small = (whole[:, rows:].astype(F32) + other[:, rows:].astype(F32)).reshape(-1)
    edges = [width, 2 * width, (2 + expert_count) * width, (2 + expert_count) * width + bucket_count * head_count]
    grad_gain1, grad_gain2, grad_router, grad_table = jnp.split(small[: edges[3]], edges[:3])
    grad_router = grad_router.reshape(expert_count, width).T
    grad_table = grad_table.reshape(head_count, bucket_count).T
    grad_query = in_order(dq_a, dq_b, 1)

    part = lax.all_to_all(part, "context", split_axis=0, concat_axis=0, tiled=True)
    grad_act = mm(grad_query, w_query, NT) + jnp.sum(part.astype(F32), axis=0).T
    grad_inputs = rms_back(grad_act, inputs_f, scale1, gain1) + grad_resid
    return (
        mixed[None].astype(BF16),
        grad_inputs[None].astype(BF16),
        grad_gain1,
        grad_w_query,
        grad_w_key,
        grad_w_value,
        grad_w_output,
        grad_table,
        grad_gain2,
        grad_router,
        grad_w_in_out,
        grad_w_out_out,
    )


def solution(mesh):
    tokens = P(("expert", "dp"), "context", None)
    return jax.shard_map(
        functools.partial(per_device, mesh.shape["context"], mesh.shape["dp"]),
        mesh=mesh,
        in_specs=(
            tokens, tokens, P(), P(), P(), P(), P(), P(), P(), P(), P(), tokens,
            P("expert", None, None), P("expert", None, None),
        ),
        out_specs=(
            tokens, tokens, P(), P(), P(), P(), P(), P(), P(), P(),
            P("expert", None, ("context", "dp")), P("expert", ("context", "dp"), None),
        ),
        check_vma=False,
    )
```

profile of v0, /device:TPU:1, one launch (start us, length us, event | category | flops | bytes accessed | tf_op | source)
XLA Modules:
  0.0 378.3 jit_solution(6810434749459024620)
XLA Ops:
  7.2 1.1 fusion.12
  8.4 0.7 convert_element_type.132
  9.1 1.7 fusion.14.own_ref
  10.8 0.7 convert_element_type.135
  11.5 0.7 fusion.47
  12.5 0.8 pad_dynamic-slice_fusion
  13.3 0.8 convolution_bitcast_fusion
  14.2 0.7 reshape.140.win_ref
  14.9 1.3 constant_dynamic-slice_fusion
  16.2 1.5 copy.38
  17.7 2.5 copy.39
  20.2 1.5 copy.40
  21.7 2.4 copy.41
  24.1 2.4 dynamic-slice_bitcast_fusion.refs_1_.refs_5_
  26.5 35.2 %all-gather.4.cloned.1.call-done.act_ref = bf16[2048,768]{1,0:T(8,128)(2,1)} async-done(((bf16[128,768]{1,0:T(8,128)(2,1)}), bf16[2048,768]{1,0:T(8,128)(2,1)}) %all-gather.4.cloned.1.call-update) | async-done | bytes 3145744 | tf_op jit(solution)/shard_map/all_gather | solution.py:488
  61.7 30.1 %attend.1 = (bf16[128,768]{1,0:T(8,128)(2,1)}, bf16[2048,768]{1,0:T(8,128)(2,1)}, bf16[2048,768]{1,0:T(8,128)(2,1)}, f32[128,768]{1,0:T(8,128)}, f32[128,768]{1,0:T(8,128)}, /*index=5*/bf16[6,256,2048]{2,1,0:T(8,128)(2,1)}) custom-call(bf16[2048,768]{1,0:T(8,128)(2,1)} %all-gather.4.cloned.1.call-done.act_ref, bf16[128,768]{1,0:T(8,128)(2,1)} %fusion.14.own_ref, ...), custom_call_target="tpu_custom_call" | custom-call | flops 6442450944 | bytes 25165824 | tf_op jit(solution)/shard_map/attend/pallas_call | solution.py:116
  91.9 1.5 multiply_reduce_fusion.2
  94.3 14.3 %all_to_all.20 = bf16[4,40,1536]{2,1,0:T(8,128)(2,1)} all-to-all(bf16[4,40,1536]{2,1,0:T(8,128)(2,1)S(1)} %bitcast.86), channel_id=1, replica_groups=mesh['expert'=4,'context'=16,'dp'=2] {'expert'}, dimensions={0} | all-to-all | bytes 983040 | tf_op jit(solution)/shard_map/all_to_all | solution.py:528
  108.7 8.5 %expert_both.1 = bf16[160,1536]{1,0:T(8,128)(2,1)} custom-call(bf16[160,1536]{1,0:T(8,128)(2,1)} %bitcast.12.rows_ref.refs_0_.ready_ref, bf16[768,3072]{1,0:T(8,128)(2,1)} %bitcast.99, bf16[3072,768]{1,0:T(8,128)(2,1)} %bitcast.100), custom_call_target="tpu_custom_call" | custom-call | flops 3019898880 | bytes 9437184 | tf_op jit(solution)/shard_map/expert_both/pallas_call | solution.py:387
  117.1 4.4 %all-to-all-start.1 = ((bf16[4,40,1536]{2,1,0:T(8,128)(2,1)}), bf16[4,40,1536]{2,1,0:T(8,128)(2,1)S(1)}, u32[]{:S(2)}, u32[]{:S(2)}) async-start(bf16[4,40,1536]{2,1,0:T(8,128)(2,1)} %bitcast.98), calls=%async_computation.1 | async-start | bytes 983040 | tf_op jit(solution)/shard_map/all_to_all | solution.py:532
  122.1 1.7 collective-permute-start.2
  124.5 6.2 %all-to-all-done.1 = bf16[4,40,1536]{2,1,0:T(8,128)(2,1)S(1)} async-done(((bf16[4,40,1536]{2,1,0:T(8,128)(2,1)}), bf16[4,40,1536]{2,1,0:T(8,128)(2,1)S(1)}, u32[]{:S(2)}, u32[]{:S(2)}) %all-to-all-start.1) | async-done | bytes 491552 | tf_op jit(solution)/shard_map/all_to_all | solution.py:532
  131.1 0.8 fusion.11
  133.0 1.2 fusion.3.do_ref
  134.6 1.0 collective-permute-start.4
  135.6 15.9 %attend_back.3 = (bf16[128,384]{1,0:T(8,128)(2,1)}, bf16[2,384,2048]{2,1,0:T(8,128)(2,1)}, bf16[3,768,384]{2,1,0:T(8,128)(2,1)}, f32[1,768]{1,0:T(1,128)}, f32[3,2,2176]{2,1,0:T(2,128)}) custom-call(s32[1]{0:T(128)S(6)} %sub.41.half_ref, bf16[6,256,2048]{2,1,0:T(8,128)(2,1)} %get-tuple-element.35.p_ref, bf16[128,768]{1,0:T(8,128)(2,1)} %fusion.3.do_ref, ...), custom_call_target="tpu_custom_call" | custom-call | flops 6442450944 | bytes 14155776 | tf_op jit(solution)/shard_map/attend_back/pallas_call | solution.py:217
  151.6 1.2 convolution_convert_fusion.2.mine_out_ref
  152.8 8.6 %expert_grads.1.ready_ref = bf16[4,2,2,96,768]{4,3,2,1,0:T(8,128)(2,1)} custom-call(s32[2]{0:T(128)} %pad_add_fusion.place_ref, bf16[160,1536]{1,0:T(8,128)(2,1)} %bitcast.12.rows_ref.refs_0_.ready_ref, bf16[160,1536]{1,0:T(8,128)(2,1)} %collective-permute-done.refs_1_, bf16[160,1536]{1,0:T(8,128)(2,1)} %collective-permute-done.1.refs_2_, ...), custom_call_target="tpu_custom_call" | custom-call | flops 3019898880 | bytes 4718592 | tf_op jit(solution)/shard_map/expert_grads/pallas_call | solution.py:427
  161.4 15.9 %attend_back.2 = (bf16[128,384]{1,0:T(8,128)(2,1)}, bf16[2,384,2048]{2,1,0:T(8,128)(2,1)}, bf16[3,768,384]{2,1,0:T(8,128)(2,1)}, f32[1,768]{1,0:T(1,128)}, f32[3,2,2176]{2,1,0:T(2,128)}) custom-call(s32[1]{0:T(128)} %bitcast.18.half_ref.core_ref, bf16[6,256,2048]{2,1,0:T(8,128)(2,1)} %get-tuple-element.35.p_ref, bf16[128,768]{1,0:T(8,128)(2,1)} %fusion.3.do_ref, ...), custom_call_target="tpu_custom_call" | custom-call | flops 6442450944 | bytes 14155776 | tf_op jit(solution)/shard_map/attend_back/pallas_call | solution.py:217
  177.3 0.8 broadcast_select_fusion.3
  178.7 0.7 add_reduce_fusion
  179.4 0.8 reshape.148.small_ref
  180.2 0.8 copy-done.8
  181.0 4.5 %merge_halves.1 = bf16[16,208,384]{2,1,0:T(8,128)(2,1)} custom-call(bf16[3,768,384]{2,1,0:T(8,128)(2,1)} %get-tuple-element.44.mine_ref, bf16[3,768,384]{2,1,0:T(8,128)(2,1)} %collective-permute-done.3.other_ref, bf16[768,384]{1,0:T(8,128)(2,1)} %convolution_convert_fusion.2.mine_out_ref, bf16[768,384]{1,0:T(8,128)(2,1)} %copy-done.8, ...), custom_call_target="tpu_custom_call" | custom-call | tf_op jit(solution)/shard_map/merge_halves/pallas_call | solution.py:312
  185.5 4.5 %all-to-all-start.2 = ((bf16[16,208,384]{2,1,0:T(8,128)(2,1)}), bf16[16,208,384]{2,1,0:T(8,128)(2,1)}, u32[]{:S(2)}, u32[]{:S(2)}) async-start(bf16[16,208,384]{2,1,0:T(8,128)(2,1)} %merge_halves.1), calls=%async_computation.2 | async-start | bytes 5111808 | tf_op jit(solution)/shard_map/all_to_all | solution.py:593
  190.0 10.6 %spread.1 = bf16[16,768,128]{2,1,0:T(8,128)(2,1)} custom-call(s32[1]{0:T(128)} %bitcast.18.half_ref.core_ref, bf16[768,768]{1,0:T(8,128)(2,1)} %wkb_ref.1, bf16[768,768]{1,0:T(8,128)(2,1)} %wvb_ref.1, bf16[2,384,2048]{2,1,0:T(8,128)(2,1)} %get-tuple-element.42.a_ref, bf16[768,768]{1,0:T(8,128)(2,1)} %wkb_ref.1, bf16[768,768]{1,0:T(8,128)(2,1)} %wvb_ref.1, ...), custom_call_target="tpu_custom_call" | custom-call | flops 4831838208 | bytes 9437184 | tf_op jit(solution)/shard_map/spread/pallas_call | solution.py:274
  200.7 28.2 %all-to-all-done.2 = bf16[16,208,384]{2,1,0:T(8,128)(2,1)} async-done(((bf16[16,208,384]{2,1,0:T(8,128)(2,1)}), bf16[16,208,384]{2,1,0:T(8,128)(2,1)}, u32[]{:S(2)}, u32[]{:S(2)}) %all-to-all-start.2) | async-done | bytes 2555936 | tf_op jit(solution)/shard_map/all_to_all | solution.py:593
  228.9 2.1 reduce_sum.110
  231.1 2.1 collective-permute-start.6
  233.2 2.0 collective-permute-done.7
  235.2 1.6 collective-permute-done.6
  236.8 4.1 %collective-permute-done.5 = bf16[208,384]{1,0:T(8,128)(2,1)S(1)} collective-permute-done((bf16[208,384]{1,0:T(8,128)(2,1)S(1)}, bf16[208,384]{1,0:T(8,128)(2,1)S(1)}, u32[]{:S(2)}, u32[]{:S(2)}) %collective-permute-start.5) | collective-permute-done | bytes 159776 | tf_op jit(solution)/shard_map/ppermute | solution.py:605
  240.9 0.8 add_convert_fusion.1
  241.7 4.5 %all-to-all-start.3 = ((bf16[16,768,128]{2,1,0:T(8,128)(2,1)}), bf16[16,768,128]{2,1,0:T(8,128)(2,1)}, u32[]{:S(2)}, u32[]{:S(2)}) async-start(bf16[16,768,128]{2,1,0:T(8,128)(2,1)} %spread.1), calls=%async_computation.3 | async-start | bytes 6291456 | tf_op jit(solution)/shard_map/all_to_all | solution.py:617
  246.2 61.8 %all-gather.6.cloned.1.call-done = bf16[3328,384]{1,0:T(8,128)(2,1)} async-done(((bf16[208,384]{1,0:T(8,128)(2,1)}), bf16[3328,384]{1,0:T(8,128)(2,1)}) %all-gather.6.cloned.1.call-update) | async-done | bytes 2555920 | tf_op jit(solution)/shard_map/all_gather | solution.py:606
  308.0 1.4 collective-permute-start.8
  309.4 1.6 slice_bitcast_fusion.7
  311.0 1.4 collective-permute-start.9
  312.3 2.0 collective-permute-start.15
  314.4 2.1 collective-permute-start.13
  316.5 15.8 %collective-permute-done.9 = bf16[2,96,768]{2,1,0:T(8,128)(2,1)S(1)} collective-permute-done((bf16[2,96,768]{2,1,0:T(8,128)(2,1)S(1)}, bf16[2,96,768]{2,1,0:T(8,128)(2,1)S(1)}, u32[]{:S(2)}, u32[]{:S(2)}) %collective-permute-start.9) | collective-permute-done | bytes 294944 | tf_op jit(solution)/shard_map/ppermute | solution.py:549
  332.3 1.6 collective-permute-start.12
  333.9 2.0 collective-permute-start.10
  336.0 5.6 %collective-permute-done.12 = bf16[2,96,768]{2,1,0:T(8,128)(2,1)S(1)} collective-permute-done((bf16[2,96,768]{2,1,0:T(8,128)(2,1)S(1)}, bf16[2,96,768]{2,1,0:T(8,128)(2,1)S(1)}, u32[]{:S(2)}, u32[]{:S(2)}) %collective-permute-start.12) | collective-permute-done | bytes 294944 | tf_op jit(solution)/shard_map/ppermute | solution.py:549
  341.6 8.5 %collective-permute-done.11 = bf16[2,96,768]{2,1,0:T(8,128)(2,1)S(1)} collective-permute-done((bf16[2,96,768]{2,1,0:T(8,128)(2,1)S(1)}, bf16[2,96,768]{2,1,0:T(8,128)(2,1)S(1)}, u32[]{:S(2)}, u32[]{:S(2)}) %collective-permute-start.11) | collective-permute-done | bytes 294944 | tf_op jit(solution)/shard_map/ppermute | solution.py:549
  350.1 5.3 %collective-permute-done.10 = bf16[2,96,768]{2,1,0:T(8,128)(2,1)S(1)} collective-permute-done((bf16[2,96,768]{2,1,0:T(8,128)(2,1)S(1)}, bf16[2,96,768]{2,1,0:T(8,128)(2,1)S(1)}, u32[]{:S(2)}, u32[]{:S(2)}) %collective-permute-start.10) | collective-permute-done | bytes 294944 | tf_op jit(solution)/shard_map/ppermute | solution.py:549
  355.4 1.3 fusion.9
  356.6 0.8 fusion.66
  357.5 2.4 convert_reduce_fusion
  360.1 0.6 fusion.15
  360.8 0.9 fusion.32
  361.7 1.1 convert_add_fusion.2
  363.3 0.6 slice_bitcast_fusion.9
  365.1 6.4 %unpack_halves.1 = (f32[768,768]{1,0:T(8,128)}, f32[768,768]{1,0:T(8,128)}, f32[768,768]{1,0:T(8,128)}, f32[768,768]{1,0:T(8,128)}) custom-call(s32[1]{0:T(128)} %bitcast.18.half_ref.core_ref, bf16[16,208,384]{2,1,0:T(8,128)(2,1)} %bitcast.84, bf16[16,208,384]{2,1,0:T(8,128)(2,1)} %collective-permute-done.8.other_ref), custom_call_target="tpu_custom_call" | custom-call | tf_op jit(solution)/shard_map/unpack_halves/pallas_call | solution.py:344
  (89 shorter events, 7.3 us)
Async XLA Ops:
  7.2 84.7 %copy-start = (bf16[768,768]{1,0:T(8,128)(2,1)S(1)}, bf16[768,768]{1,0:T(8,128)(2,1)}, u32[]{:S(2)}) copy-start(bf16[768,768]{1,0:T(8,128)(2,1)} %param.20) | copy-start | bytes 3538948
  7.2 54.5 %all-gather.4.cloned.1.call-start = ((), (), s32[]{:S(2)}) async-start(), calls=%async_computation.4 | async-start | bytes 3342336 | tf_op jit(solution)/shard_map/all_gather | solution.py:488
  17.7 2.5 copy-start.7
  20.2 3.9 %copy-start.14 = (s32[1,128,1]{1,2,0:T(1,128)S(1)}, s32[1,128,1]{1,2,0:T(1,128)}, u32[]{:S(2)}) copy-start(s32[1,128,1]{1,2,0:T(1,128)} %param.25) | copy-start | bytes 1540
  61.7 30.2 %copy-start.2 = (bf16[1,128,768]{2,1,0:T(8,128)(2,1)S(1)}, bf16[1,128,768]{2,1,0:T(8,128)(2,1)}, u32[]{:S(2)}) copy-start(bf16[1,128,768]{2,1,0:T(8,128)(2,1)} %param.14) | copy-start | bytes 589828
  91.9 1.5 copy-start.13
  91.9 2.0 copy-start.6
  117.1 13.6 %all-to-all-start.1 = ((bf16[4,40,1536]{2,1,0:T(8,128)(2,1)}), bf16[4,40,1536]{2,1,0:T(8,128)(2,1)S(1)}, u32[]{:S(2)}, u32[]{:S(2)}) async-start(bf16[4,40,1536]{2,1,0:T(8,128)(2,1)} %bitcast.98), calls=%async_computation.1 | async-start | bytes 983040 | tf_op jit(solution)/shard_map/all_to_all | solution.py:532
  122.1 30.7 %collective-permute-start.2 = (bf16[160,1536]{1,0:T(8,128)(2,1)}, bf16[160,1536]{1,0:T(8,128)(2,1)}, u32[]{:S(2)}, u32[]{:S(2)}) collective-permute-start(bf16[160,1536]{1,0:T(8,128)(2,1)} %bitcast.12.rows_ref.refs_0_.ready_ref), channel_id=1, source_target_pairs={{0,24},{2,26},{4,28},{6,30},{8,0},{10,2},{12,4},{14,6},{16,8},{18,... | collective-permute-start | bytes 1474568 | tf_op jit(solution)/shard_map/ppermute | solution.py:482
  123.8 29.1 %collective-permute-start.1 = (bf16[160,1536]{1,0:T(8,128)(2,1)}, bf16[160,1536]{1,0:T(8,128)(2,1)}, u32[]{:S(2)}, u32[]{:S(2)}) collective-permute-start(bf16[160,1536]{1,0:T(8,128)(2,1)} %bitcast.12.rows_ref.refs_0_.ready_ref), channel_id=1, source_target_pairs={{0,16},{2,18},{4,20},{6,22},{8,24},{10,26},{12,28},{14,30},{16,0},... | collective-permute-start | bytes 1474568 | tf_op jit(solution)/shard_map/ppermute | solution.py:482
  124.3 28.5 %collective-permute-start = (bf16[160,1536]{1,0:T(8,128)(2,1)}, bf16[160,1536]{1,0:T(8,128)(2,1)}, u32[]{:S(2)}, u32[]{:S(2)}) collective-permute-start(bf16[160,1536]{1,0:T(8,128)(2,1)} %bitcast.12.rows_ref.refs_0_.ready_ref), channel_id=1, source_target_pairs={{0,8},{2,10},{4,12},{6,14},{8,16},{10,18},{12,20},{14,22},{16,24},... | collective-permute-start | bytes 1474568 | tf_op jit(solution)/shard_map/ppermute | solution.py:482
  131.1 1.9 copy-start.9
  132.4 1.8 copy-start.4
  134.6 45.6 %collective-permute-start.4 = (bf16[768,384]{1,0:T(8,128)(2,1)S(1)}, bf16[768,384]{1,0:T(8,128)(2,1)S(1)}, u32[]{:S(2)}, u32[]{:S(2)}) collective-permute-start(bf16[768,384]{1,0:T(8,128)(2,1)S(1)} %convolution_convert_fusion.1), channel_id=1, source_target_pairs={{0,32},{32,0},{64,96},{96,64},{1,33},{33,1},{65,97},{97,65},{2,34}... | collective-permute-start | bytes 1769480 | tf_op jit(solution)/shard_map/ppermute | solution.py:572
  135.6 16.0 %copy-start.5 = (f32[128,768]{1,0:T(8,128)S(1)}, f32[128,768]{1,0:T(8,128)}, u32[]{:S(2)}) copy-start(f32[128,768]{1,0:T(8,128)} %get-tuple-element.34.o_ref) | copy-start | bytes 1179652
  151.5 28.7 %collective-permute-start.3 = (bf16[3,768,384]{2,1,0:T(8,128)(2,1)}, bf16[3,768,384]{2,1,0:T(8,128)(2,1)}, u32[]{:S(2)}, u32[]{:S(2)}) collective-permute-start(bf16[3,768,384]{2,1,0:T(8,128)(2,1)} %get-tuple-element.45), channel_id=1, source_target_pairs={{0,32},{32,0},{64,96},{96,64},{1,33},{33,1},{65,97},{97,65},{2,34}... | collective-permute-start | bytes 5308424 | tf_op jit(solution)/shard_map/ppermute | solution.py:578
  161.4 15.9 %copy-start.12 = (f32[3,2,2176]{2,1,0:T(2,128)S(1)}, f32[3,2,2176]{2,1,0:T(2,128)}, u32[]{:S(2)}) copy-start(f32[3,2,2176]{2,1,0:T(2,128)} %get-tuple-element.49) | copy-start | bytes 156676
  161.4 17.3 %copy-start.16 = (f32[1,768]{1,0:T(1,128)S(1)}, f32[1,768]{1,0:T(1,128)}, u32[]{:S(2)}) copy-start(f32[1,768]{1,0:T(1,128)} %get-tuple-element.46) | copy-start | bytes 9220
  161.4 18.0 %copy-start.15 = (bf16[768]{0:T(1024)(128)(2,1)S(1)}, bf16[768]{0:T(1024)(128)(2,1)}, u32[]{:S(2)}) copy-start(bf16[768]{0:T(1024)(128)(2,1)} %param.16) | copy-start | bytes 4612
  180.2 0.8 copy-start.8
  185.5 43.4 %all-to-all-start.2 = ((bf16[16,208,384]{2,1,0:T(8,128)(2,1)}), bf16[16,208,384]{2,1,0:T(8,128)(2,1)}, u32[]{:S(2)}, u32[]{:S(2)}) async-start(bf16[16,208,384]{2,1,0:T(8,128)(2,1)} %merge_halves.1), calls=%async_computation.2 | async-start | bytes 5111808 | tf_op jit(solution)/shard_map/all_to_all | solution.py:593
  190.0 118.0 %all-gather.6.cloned.1.call-start = ((), (), s32[]{:S(2)}) async-start(), calls=%async_computation.5 | async-start | bytes 2715648 | tf_op jit(solution)/shard_map/all_gather | solution.py:606
  231.0 4.2 %collective-permute-start.7 = (bf16[208,384]{1,0:T(8,128)(2,1)S(1)}, bf16[208,384]{1,0:T(8,128)(2,1)S(1)}, u32[]{:S(2)}, u32[]{:S(2)}) collective-permute-start(bf16[208,384]{1,0:T(8,128)(2,1)S(1)} %reduce_sum.110), channel_id=1, source_target_pairs={{0,65},{1,0},{32,97},{33,32},{64,1},{65,64},{96,33},{97,96},{2,67}... | collective-permute-start | bytes 479240 | tf_op jit(solution)/shard_map/ppermute | solution.py:605
  231.1 5.7 %collective-permute-start.6 = (bf16[208,384]{1,0:T(8,128)(2,1)S(1)}, bf16[208,384]{1,0:T(8,128)(2,1)S(1)}, u32[]{:S(2)}, u32[]{:S(2)}) collective-permute-start(bf16[208,384]{1,0:T(8,128)(2,1)S(1)} %reduce_sum.110), channel_id=1, source_target_pairs={{0,64},{1,65},{32,96},{33,97},{64,0},{65,1},{96,32},{97,33},{2,66}... | collective-permute-start | bytes 479240 | tf_op jit(solution)/shard_map/ppermute | solution.py:605
  233.2 7.7 %collective-permute-start.5 = (bf16[208,384]{1,0:T(8,128)(2,1)S(1)}, bf16[208,384]{1,0:T(8,128)(2,1)S(1)}, u32[]{:S(2)}, u32[]{:S(2)}) collective-permute-start(bf16[208,384]{1,0:T(8,128)(2,1)S(1)} %reduce_sum.110), channel_id=1, source_target_pairs={{0,1},{1,64},{32,33},{33,96},{64,65},{65,0},{96,97},{97,32},{2,3},... | collective-permute-start | bytes 479240 | tf_op jit(solution)/shard_map/ppermute | solution.py:605
  241.7 115.8 %all-to-all-start.3 = ((bf16[16,768,128]{2,1,0:T(8,128)(2,1)}), bf16[16,768,128]{2,1,0:T(8,128)(2,1)}, u32[]{:S(2)}, u32[]{:S(2)}) async-start(bf16[16,768,128]{2,1,0:T(8,128)(2,1)} %spread.1), calls=%async_computation.3 | async-start | bytes 6291456 | tf_op jit(solution)/shard_map/all_to_all | solution.py:617
  308.0 28.0 %copy-start.10 = (bf16[128,384]{1,0:T(8,128)(2,1)S(1)}, bf16[128,384]{1,0:T(8,128)(2,1)}, u32[]{:S(2)}) copy-start(bf16[128,384]{1,0:T(8,128)(2,1)} %get-tuple-element.41) | copy-start | bytes 294916
  308.0 28.0 %copy-start.11 = (bf16[128,384]{1,0:T(8,128)(2,1)S(1)}, bf16[128,384]{1,0:T(8,128)(2,1)}, u32[]{:S(2)}) copy-start(bf16[128,384]{1,0:T(8,128)(2,1)} %get-tuple-element.40) | copy-start | bytes 294916
  308.0 53.7 %collective-permute-start.8 = (bf16[16,208,384]{2,1,0:T(8,128)(2,1)}, bf16[16,208,384]{2,1,0:T(8,128)(2,1)}, u32[]{:S(2)}, u32[]{:S(2)}) collective-permute-start(bf16[16,208,384]{2,1,0:T(8,128)(2,1)} %bitcast.82), channel_id=1, source_target_pairs={{0,32},{32,0},{64,96},{96,64},{1,33},{33,1},{65,97},{97,65},{2,34}... | collective-permute-start | bytes 7667720 | tf_op jit(solution)/shard_map/ppermute | solution.py:607
  311.0 21.3 %collective-permute-start.9 = (bf16[2,96,768]{2,1,0:T(8,128)(2,1)S(1)}, bf16[2,96,768]{2,1,0:T(8,128)(2,1)S(1)}, u32[]{:S(2)}, u32[]{:S(2)}) collective-permute-start(bf16[2,96,768]{2,1,0:T(8,128)(2,1)S(1)} %get-tuple-element.58), channel_id=1, source_target_pairs={{0,1},{1,0},{2,3},{3,2},{4,5},{5,4},{6,7},{7,6},{8,9},{9,8},{10,11... | collective-permute-start | bytes 884744 | tf_op jit(solution)/shard_map/ppermute | solution.py:549
  312.3 21.6 %collective-permute-start.15 = (bf16[2,96,768]{2,1,0:T(8,128)(2,1)S(1)}, bf16[2,96,768]{2,1,0:T(8,128)(2,1)S(1)}, u32[]{:S(2)}, u32[]{:S(2)}) collective-permute-start(bf16[2,96,768]{2,1,0:T(8,128)(2,1)S(1)} %get-tuple-element.59), channel_id=1, source_target_pairs={{0,7},{1,6},{2,1},{3,0},{4,3},{5,2},{6,5},{7,4},{8,15},{9,14},{10,... | collective-permute-start | bytes 884744 | tf_op jit(solution)/shard_map/ppermute | solution.py:549
  314.3 19.6 %collective-permute-start.14 = (bf16[2,96,768]{2,1,0:T(8,128)(2,1)S(1)}, bf16[2,96,768]{2,1,0:T(8,128)(2,1)S(1)}, u32[]{:S(2)}, u32[]{:S(2)}) collective-permute-start(bf16[2,96,768]{2,1,0:T(8,128)(2,1)S(1)} %get-tuple-element.60), channel_id=1, source_target_pairs={{0,6},{1,7},{2,0},{3,1},{4,2},{5,3},{6,4},{7,5},{8,14},{9,15},{10,... | collective-permute-start | bytes 884744 | tf_op jit(solution)/shard_map/ppermute | solution.py:549
  314.4 21.6 %collective-permute-start.13 = (bf16[2,96,768]{2,1,0:T(8,128)(2,1)S(1)}, bf16[2,96,768]{2,1,0:T(8,128)(2,1)S(1)}, u32[]{:S(2)}, u32[]{:S(2)}) collective-permute-start(bf16[2,96,768]{2,1,0:T(8,128)(2,1)S(1)} %get-tuple-element.61), channel_id=1, source_target_pairs={{0,5},{1,4},{2,7},{3,6},{4,1},{5,0},{6,3},{7,2},{8,13},{9,12},{10,... | collective-permute-start | bytes 884744 | tf_op jit(solution)/shard_map/ppermute | solution.py:549
  332.3 9.2 %collective-permute-start.12 = (bf16[2,96,768]{2,1,0:T(8,128)(2,1)S(1)}, bf16[2,96,768]{2,1,0:T(8,128)(2,1)S(1)}, u32[]{:S(2)}, u32[]{:S(2)}) collective-permute-start(bf16[2,96,768]{2,1,0:T(8,128)(2,1)S(1)} %get-tuple-element.62), channel_id=1, source_target_pairs={{0,4},{1,5},{2,6},{3,7},{4,0},{5,1},{6,2},{7,3},{8,12},{9,13},{10,... | collective-permute-start | bytes 884744 | tf_op jit(solution)/shard_map/ppermute | solution.py:549
  333.9 16.1 %collective-permute-start.11 = (bf16[2,96,768]{2,1,0:T(8,128)(2,1)S(1)}, bf16[2,96,768]{2,1,0:T(8,128)(2,1)S(1)}, u32[]{:S(2)}, u32[]{:S(2)}) collective-permute-start(bf16[2,96,768]{2,1,0:T(8,128)(2,1)S(1)} %get-tuple-element.63), channel_id=1, source_target_pairs={{0,3},{1,2},{2,5},{3,4},{4,7},{5,6},{6,1},{7,0},{8,11},{9,10},{10,... | collective-permute-start | bytes 884744 | tf_op jit(solution)/shard_map/ppermute | solution.py:549
  333.9 21.5 %collective-permute-start.10 = (bf16[2,96,768]{2,1,0:T(8,128)(2,1)S(1)}, bf16[2,96,768]{2,1,0:T(8,128)(2,1)S(1)}, u32[]{:S(2)}, u32[]{:S(2)}) collective-permute-start(bf16[2,96,768]{2,1,0:T(8,128)(2,1)S(1)} %get-tuple-element.64), channel_id=1, source_target_pairs={{0,2},{1,3},{2,4},{3,5},{4,6},{5,7},{6,0},{7,1},{8,10},{9,11},{10,... | collective-permute-start | bytes 884744 | tf_op jit(solution)/shard_map/ppermute | solution.py:549
  357.5 2.6 copy-start.3
  364.5 7.0 %copy-start.1 = (bf16[768,768]{1,0:T(8,128)(2,1)S(1)}, bf16[768,768]{1,0:T(8,128)(2,1)}, u32[]{:S(2)}) copy-start(bf16[768,768]{1,0:T(8,128)(2,1)} %param.20) | copy-start | bytes 3538948
Sparse Core Ops, SparseCore 0:
  10.9 50.7 all-gather.3
  241.8 66.1 all-gather.5
where the time goes:
time: 380 us; the launch traced here: 378 us
  waiting for transfers between devices  174 us (46%)
  Pallas kernels  100 us (26%)
  starting transfers between devices  29.7 us (8%)
  local copies, waits for them, and re-layouts  20.1 us (5%)
  other arithmetic  17 us (4%)
  between operations  14.5 us (4%)
  blocking collectives  14.3 us (4%)
  matrix products  7.81 us (2%)
    all_gather x1, waiting for transfers between devices, per_device(): whole = lax.all_gather(total.astype(BF16), 'context', axis=0)  61.8 us
    all_gather x1, waiting for transfers between devices, per_device(): act_all = lax.all_gather(act, 'context', axis=0, tiled=True)  35.2 us
    ppermute x7, waiting for transfers between devices, per_device(): moved = lax.ppermute(shares[step, flip], ('context', 'dp'), route_pairs)  35.2 us
    pallas_call x2, Pallas kernels, attend_back(): pl.pallas_call(attend_back_kernel, grid_spec=pltpu.PrefetchScalarGridSpec...  31.8 us
    pallas_call x1, Pallas kernels, attend(): pl.pallas_call(attend_kernel, grid=(pairs,), in_specs=[whole(length), who...  30.1 us
    all_to_all x1, waiting for transfers between devices, per_device(): lax.all_to_all(merged, 'context', split_axis=0, concat_axis=0, tiled=True)  28.2 us
    all_to_all x1, blocking collectives, per_device(): lax.all_to_all(going, 'expert', split_axis=0, concat_axis=0, tiled=True)  14.3 us
    pallas_call x1, Pallas kernels, spread(): pl.pallas_call(spread_kernel, grid_spec=pltpu.PrefetchScalarGridSpec(num_...  10.6 us
  transfers between devices with their start and end apart: 21, of which 11 were waited for; matrix products, arithmetic and copies ran while one was open for 8% of the time, Pallas kernels for 13%

commit v1 on v0

--- a/solution.py
+++ b/solution.py
@@ -88,18 +88,22 @@
             rows = rows_of(head, r)
             s = s_ref[rows, :] + bands[head][:, :length]
             s_ref[rows, :] = s
-            m_ref[rows, :] = jnp.broadcast_to(jnp.max(s, axis=1, keepdims=True), (16, lanes))
+            tops = [s[:, c : c + lanes] for c in range(0, length, lanes)]
+            while len(tops) > 1:
+                tops = [jnp.maximum(a, b) for a, b in zip(tops[::2], tops[1::2])]
+            m_ref[rows, :] = tops[0]
         return tuple(pltpu.roll(band, 16, 1) for band in bands)
 
     def exponents(r, carry):
-        for head in range(2):
-            rows = rows_of(head, r)
+        for part in range(4):
+            rows = rows_of(0, 4 * r + part)
             top = jnp.concatenate([m_ref[rows, :]] * (length // lanes), 1)
             p_ref[0, rows, :] = jnp.exp(s_ref[rows, :] - top).astype(BF16)
         return carry
 
     lax.fori_loop(0, tok // 16, add_bias, (first_band(0), first_band(1)))
-    lax.fori_loop(0, tok // 16, exponents, 0)
+    m_ref[...] = jnp.broadcast_to(jnp.max(m_ref[...], axis=1, keepdims=True), m_ref.shape)
+    lax.fori_loop(0, tok // 32, exponents, 0)
     summed = mm(p_ref[0], ext_ref[...])
     inverse = 1.0 / join_pair(summed[:, lanes:], size)
     inv_ref[...] = inverse
@@ -255,7 +259,8 @@
     )(half, probs, grad_heads, heads, query, key, value, act_all, act, *turned, ready)
 
 
-def spread_kernel(half_ref, wka_ref, wva_ref, a_ref, wkb_ref, wvb_ref, b_ref, out_ref):
+def spread_kernel(half_ref, wka_ref, wva_ref, a_ref, wkb_ref, wvb_ref, b_ref, *refs):
+    out_ref = refs[-1]
     tok = out_ref.shape[2]
     found = mm(jnp.concatenate([wka_ref[...], wva_ref[...]], 1), jnp.concatenate([a_ref[0], a_ref[1]], 0))
     found += mm(jnp.concatenate([wkb_ref[...], wvb_ref[...]], 1), jnp.concatenate([b_ref[0], b_ref[1]], 0))
@@ -264,7 +269,7 @@
         out_ref[i] = found[:, i * tok : (i + 1) * tok]
 
 
-def spread(half, w_key, w_value, terms_a, terms_b, tok):
+def spread(half, w_key, w_value, terms_a, terms_b, tok, ready):
     width = w_key.shape[0]
     length = terms_a.shape[2]
     cols = width // 2
@@ -276,7 +281,8 @@
         grid_spec=pltpu.PrefetchScalarGridSpec(
             num_scalar_prefetch=1,
             grid=(length // (2 * tok),),
-            in_specs=[weight_a, weight_a, terms, weight_b, weight_b, terms],
+            in_specs=[weight_a, weight_a, terms, weight_b, weight_b, terms]
+            + [pl.BlockSpec(memory_space=pl.ANY)] * len(ready),
             out_specs=pl.BlockSpec((2, width, tok), lambda c, h: (c, 0, 0)),
         ),
         out_shape=jax.ShapeDtypeStruct((length // tok, width, tok), BF16),
@@ -285,7 +291,7 @@
             flops=4 * length * width * width, bytes_accessed=6 * length * width, transcendentals=0
         ),
         name="spread",
-    )(half, w_key, w_value, terms_a, w_key, w_value, terms_b)
+    )(half, w_key, w_value, terms_a, w_key, w_value, terms_b, *ready)
 
 
 def merge_kernel(mine_ref, other_ref, mine_out_ref, other_out_ref, small_ref, out_ref):
@@ -404,11 +410,17 @@
 
 
 def expert_grad_kernel(place_ref, *refs):
-    row_refs, (wint_ref, wout_ref, out_ref) = refs[:-3], refs[-3:]
+    row_refs, (wint_ref, wout_ref, out_ref, rows_ref) = refs[:-4], refs[-4:]
     width = wint_ref.shape[1]
-    rows = jnp.concatenate([ref[...] for ref in row_refs], 0)
-    sent = rows[:, :width]
-    grad = rows[:, width:]
+    count = row_refs[0].shape[0]
+
+    @pl.when(pl.program_id(0) == 0)
+    def _():
+        for i, ref in enumerate(row_refs):
+            rows_ref[i * count : (i + 1) * count, :] = ref[...]
+
+    sent = rows_ref[:, :width]
+    grad = rows_ref[:, width:]
     hidden, slope = gelu_parts(mm(wint_ref[...], sent, NT))
     grad_pre = (mm(wout_ref[...], grad, NT) * slope).astype(BF16)
     found = (mm(grad_pre, sent).astype(BF16), mm(hidden.astype(BF16), grad).astype(BF16))
@@ -434,6 +446,7 @@
                 (1, 2, 2, chunk // 2, width),
                 lambda c, place: (lax.rem(c + side - place[0], side), 0, 0, 0, 0),
             ),
+            scratch_shapes=[pltpu.VMEM((count, 2 * width), BF16)],
         ),
         out_shape=jax.ShapeDtypeStruct((side, 2, 2, chunk // 2, width), BF16),
         compiler_params=pltpu.CompilerParams(vmem_limit_bytes=56 * MIB),
@@ -577,7 +590,6 @@
     dq_a, terms_a, grads_a, gain_a, diag_a = back(1 - core, ready=arrived)
     other = lax.ppermute(grads_a, "expert", swap)
     dq_b, terms_b, grads_b, gain_b, diag_b = back(core, ready=shares)
-    part = spread(core, w_key, w_value, terms_b, terms_a, tok_count)
     low = core[0] == 0
     in_order = lambda a, b, axis: jnp.concatenate([jnp.where(low, b, a), jnp.where(low, a, b)], axis)
     diagonals = in_order(diag_a, diag_b, 0)
@@ -590,6 +602,7 @@
     )
     small = jnp.pad(small, (0, ctx_count * 16 * cols - small.size)).astype(BF16)
     merged = merge_halves(grads_b, other, both_out[1], other_out, small.reshape(ctx_count, 16, cols))
+    part = spread(core, w_key, w_value, terms_b, terms_a, tok_count, (expert_sum, merged))
     merged = lax.all_to_all(merged, "context", split_axis=0, concat_axis=0, tiled=True)
     merged = jnp.sum(merged.astype(F32), axis=0).astype(BF16)
     part, merged = lax.optimization_barrier((part, merged))

time: 380 us -> 375 us (0.987)
  waiting for transfers between devices: 174 us -> 166 us
  starting transfers between devices: 29.7 us -> 35.6 us
    all_to_all x1, waiting for transfers between devices: 28.2 us -> 0.01 us  [per_device(): lax.all_to_all(merged, 'context', split_axis=0, concat_axis=0, tiled=True)]
    ppermute x7, waiting for transfers between devices: 35.2 us -> 55.1 us  [per_device(): moved = lax.ppermute(shares[step, flip], ('context', 'dp'), route_pairs)]
  transfers between devices with their start and end apart: 21 -> 21, of which waited for: 11 -> 11; matrix products, arithmetic and copies ran while one was open for 8% -> 8% of each run, Pallas kernels for 13% -> 14%
where the time goes in v1:
time: 375 us; the launch traced here: 374 us
  waiting for transfers between devices  166 us (44%)
  Pallas kernels  99 us (26%)
  starting transfers between devices  35.6 us (9%)
  local copies, waits for them, and re-layouts  19.7 us (5%)
  other arithmetic  16.5 us (4%)
  between operations  14.6 us (4%)
  blocking collectives  14.3 us (4%)
  matrix products  8.46 us (2%)
    all_gather x1, waiting for transfers between devices, per_device(): whole = lax.all_gather(total.astype(BF16), 'context', axis=0)  63.7 us
    ppermute x7, waiting for transfers between devices, per_device(): moved = lax.ppermute(shares[step, flip], ('context', 'dp'), route_pairs)  55.1 us
    all_gather x1, waiting for transfers between devices, per_device(): act_all = lax.all_gather(act, 'context', axis=0, tiled=True)  36.8 us
    pallas_call x2, Pallas kernels, attend_back(): pl.pallas_call(attend_back_kernel, grid_spec=pltpu.PrefetchScalarGridSpec...  31.8 us
    pallas_call x1, Pallas kernels, attend(): pl.pallas_call(attend_kernel, grid=(pairs,), in_specs=[whole(length), who...  28.6 us
    all_to_all x1, blocking collectives, per_device(): lax.all_to_all(going, 'expert', split_axis=0, concat_axis=0, tiled=True)  14.3 us
    ppermute x7, starting transfers between devices, per_device(): moved = lax.ppermute(shares[step, flip], ('context', 'dp'), route_pairs)  12 us
    pallas_call x1, Pallas kernels, spread(): pl.pallas_call(spread_kernel, grid_spec=pltpu.PrefetchScalarGridSpec(num_...  10.5 us
  transfers between devices with their start and end apart: 21, of which 11 were waited for; matrix products, arithmetic and copies ran while one was open for 8% of the time, Pallas kernels for 14%

profile of v1, /device:TPU:1, one launch (start us, length us, event | category | flops | bytes accessed | tf_op | source)
XLA Modules:
  0.0 373.7 jit_solution(44255737833280154)
XLA Ops:
  7.2 1.1 fusion.12
  8.9 0.7 convert_element_type.132
  9.6 1.7 fusion.14.own_ref
  11.4 1.4 constant_dynamic-slice_fusion
  12.7 1.5 copy.38
  14.2 0.9 pad_dynamic-slice_fusion
  15.1 1.5 convolution_bitcast_fusion
  16.6 1.6 reshape.140.win_ref
  18.2 1.5 copy.39
  19.7 1.5 copy.40
  21.2 1.5 copy.41
  23.0 2.4 dynamic-slice_bitcast_fusion.refs_1_.refs_5_
  25.4 36.8 %all-gather.4.cloned.1.call-done.act_ref = bf16[2048,768]{1,0:T(8,128)(2,1)} async-done(((bf16[128,768]{1,0:T(8,128)(2,1)}), bf16[2048,768]{1,0:T(8,128)(2,1)}) %all-gather.4.cloned.1.call-update) | async-done | bytes 3145744 | tf_op jit(solution)/shard_map/all_gather | solution.py:501
  62.2 28.6 %attend.1 = (bf16[128,768]{1,0:T(8,128)(2,1)}, bf16[2048,768]{1,0:T(8,128)(2,1)}, bf16[2048,768]{1,0:T(8,128)(2,1)}, f32[128,768]{1,0:T(8,128)}, f32[128,768]{1,0:T(8,128)}, /*index=5*/bf16[6,256,2048]{2,1,0:T(8,128)(2,1)}) custom-call(bf16[2048,768]{1,0:T(8,128)(2,1)} %all-gather.4.cloned.1.call-done.act_ref, bf16[128,768]{1,0:T(8,128)(2,1)} %fusion.14.own_ref, ...), custom_call_target="tpu_custom_call" | custom-call | flops 6442450944 | bytes 25165824 | tf_op jit(solution)/shard_map/attend/pallas_call | solution.py:120
  90.9 1.5 multiply_reduce_fusion.2
  93.3 14.3 %all_to_all.20 = bf16[4,40,1536]{2,1,0:T(8,128)(2,1)} all-to-all(bf16[4,40,1536]{2,1,0:T(8,128)(2,1)S(1)} %bitcast.86), channel_id=1, replica_groups=mesh['expert'=4,'context'=16,'dp'=2] {'expert'}, dimensions={0} | all-to-all | bytes 983040 | tf_op jit(solution)/shard_map/all_to_all | solution.py:541
  107.6 8.5 %expert_both.1 = bf16[160,1536]{1,0:T(8,128)(2,1)} custom-call(bf16[160,1536]{1,0:T(8,128)(2,1)} %bitcast.12.rows_ref.refs_0_.ready_ref, bf16[768,3072]{1,0:T(8,128)(2,1)} %bitcast.99, bf16[3072,768]{1,0:T(8,128)(2,1)} %bitcast.100), custom_call_target="tpu_custom_call" | custom-call | flops 3019898880 | bytes 9437184 | tf_op jit(solution)/shard_map/expert_both/pallas_call | solution.py:393
  116.1 4.4 %all-to-all-start.1 = ((bf16[4,40,1536]{2,1,0:T(8,128)(2,1)}), bf16[4,40,1536]{2,1,0:T(8,128)(2,1)S(1)}, u32[]{:S(2)}, u32[]{:S(2)}) async-start(bf16[4,40,1536]{2,1,0:T(8,128)(2,1)} %bitcast.98), calls=%async_computation.1 | async-start | bytes 983040 | tf_op jit(solution)/shard_map/all_to_all | solution.py:545
  121.5 2.4 collective-permute-start.1
  123.9 0.8 collective-permute-start.2
  124.7 4.9 %all-to-all-done.1 = bf16[4,40,1536]{2,1,0:T(8,128)(2,1)S(1)} async-done(((bf16[4,40,1536]{2,1,0:T(8,128)(2,1)}), bf16[4,40,1536]{2,1,0:T(8,128)(2,1)S(1)}, u32[]{:S(2)}, u32[]{:S(2)}) %all-to-all-start.1) | async-done | bytes 491552 | tf_op jit(solution)/shard_map/all_to_all | solution.py:545
  129.9 0.8 fusion.11
  131.8 1.2 fusion.3.do_ref
  133.4 1.1 collective-permute-start.11
  134.5 15.9 %attend_back.3 = (bf16[128,384]{1,0:T(8,128)(2,1)}, bf16[2,384,2048]{2,1,0:T(8,128)(2,1)}, bf16[3,768,384]{2,1,0:T(8,128)(2,1)}, f32[1,768]{1,0:T(1,128)}, f32[3,2,2176]{2,1,0:T(2,128)}) custom-call(s32[1]{0:T(128)S(6)} %sub.41.half_ref, bf16[6,256,2048]{2,1,0:T(8,128)(2,1)} %get-tuple-element.35.p_ref, bf16[128,768]{1,0:T(8,128)(2,1)} %fusion.3.do_ref, ...), custom_call_target="tpu_custom_call" | custom-call | flops 6442450944 | bytes 14155776 | tf_op jit(solution)/shard_map/attend_back/pallas_call | solution.py:221
  150.6 1.2 convolution_convert_fusion.2.mine_out_ref
  151.8 8.7 %expert_grads.1.ready_ref = bf16[4,2,2,96,768]{4,3,2,1,0:T(8,128)(2,1)} custom-call(s32[2]{0:T(128)} %pad_add_fusion.place_ref, bf16[160,1536]{1,0:T(8,128)(2,1)} %bitcast.12.rows_ref.refs_0_.ready_ref, bf16[160,1536]{1,0:T(8,128)(2,1)} %collective-permute-done.refs_1_, bf16[160,1536]{1,0:T(8,128)(2,1)} %collective-permute-done.1.refs_2_, ...), custom_call_target="tpu_custom_call" | custom-call | flops 3019898880 | bytes 4718592 | tf_op jit(solution)/shard_map/expert_grads/pallas_call | solution.py:439
  160.5 15.9 %attend_back.2 = (bf16[128,384]{1,0:T(8,128)(2,1)}, bf16[2,384,2048]{2,1,0:T(8,128)(2,1)}, bf16[3,768,384]{2,1,0:T(8,128)(2,1)}, f32[1,768]{1,0:T(1,128)}, f32[3,2,2176]{2,1,0:T(2,128)}) custom-call(s32[1]{0:T(128)} %bitcast.18.half_ref.core_ref, bf16[6,256,2048]{2,1,0:T(8,128)(2,1)} %get-tuple-element.35.p_ref, bf16[128,768]{1,0:T(8,128)(2,1)} %fusion.3.do_ref, ...), custom_call_target="tpu_custom_call" | custom-call | flops 6442450944 | bytes 14155776 | tf_op jit(solution)/shard_map/attend_back/pallas_call | solution.py:221
  176.4 0.8 broadcast_select_fusion.3
  177.8 0.7 add_reduce_fusion
  178.5 0.8 reshape.148.small_ref
  179.3 0.8 copy-done.11
  180.1 4.5 %merge_halves.1.refs_1_ = bf16[16,208,384]{2,1,0:T(8,128)(2,1)} custom-call(bf16[3,768,384]{2,1,0:T(8,128)(2,1)} %get-tuple-element.44.mine_ref, bf16[3,768,384]{2,1,0:T(8,128)(2,1)} %collective-permute-done.10.other_ref, bf16[768,384]{1,0:T(8,128)(2,1)} %convolution_convert_fusion.2.mine_out_ref, bf16[768,384]{1,0:T(8,128)(2,1)} %copy-done.11, ...), custom_call_target="tpu_custom_call" | custom-call | tf_op jit(solution)/shard_map/merge_halves/pallas_call | solution.py:318
  184.6 4.5 %all-to-all-start.2 = ((bf16[16,208,384]{2,1,0:T(8,128)(2,1)}), bf16[16,208,384]{2,1,0:T(8,128)(2,1)}, u32[]{:S(2)}, u32[]{:S(2)}) async-start(bf16[16,208,384]{2,1,0:T(8,128)(2,1)} %merge_halves.1.refs_1_), calls=%async_computation.2 | async-start | bytes 5111808 | tf_op jit(solution)/shard_map/all_to_all | solution.py:606
  189.1 1.6 slice_bitcast_fusion.7
  191.2 1.2 collective-permute-start.4
  192.4 2.0 collective-permute-start.5
  194.4 1.5 collective-permute-start.6
  195.9 1.6 collective-permute-start.7
  197.5 1.5 collective-permute-done.3
  199.0 2.0 collective-permute-start.8
  200.9 29.1 %collective-permute-done.4 = bf16[2,96,768]{2,1,0:T(8,128)(2,1)S(1)} collective-permute-done((bf16[2,96,768]{2,1,0:T(8,128)(2,1)S(1)}, bf16[2,96,768]{2,1,0:T(8,128)(2,1)S(1)}, u32[]{:S(2)}, u32[]{:S(2)}) %collective-permute-start.4) | collective-permute-done | bytes 294944 | tf_op jit(solution)/shard_map/ppermute | solution.py:562
  230.1 3.3 collective-permute-start.9
  233.4 5.8 %collective-permute-done.5 = bf16[2,96,768]{2,1,0:T(8,128)(2,1)S(1)} collective-permute-done((bf16[2,96,768]{2,1,0:T(8,128)(2,1)S(1)}, bf16[2,96,768]{2,1,0:T(8,128)(2,1)S(1)}, u32[]{:S(2)}, u32[]{:S(2)}) %collective-permute-start.5) | collective-permute-done | bytes 294944 | tf_op jit(solution)/shard_map/ppermute | solution.py:562
  239.2 10.9 %collective-permute-done.6 = bf16[2,96,768]{2,1,0:T(8,128)(2,1)S(1)} collective-permute-done((bf16[2,96,768]{2,1,0:T(8,128)(2,1)S(1)}, bf16[2,96,768]{2,1,0:T(8,128)(2,1)S(1)}, u32[]{:S(2)}, u32[]{:S(2)}) %collective-permute-start.6) | collective-permute-done | bytes 294944 | tf_op jit(solution)/shard_map/ppermute | solution.py:562
  250.2 7.7 %collective-permute-done.7 = bf16[2,96,768]{2,1,0:T(8,128)(2,1)S(1)} collective-permute-done((bf16[2,96,768]{2,1,0:T(8,128)(2,1)S(1)}, bf16[2,96,768]{2,1,0:T(8,128)(2,1)S(1)}, u32[]{:S(2)}, u32[]{:S(2)}) %collective-permute-start.7) | collective-permute-done | bytes 294944 | tf_op jit(solution)/shard_map/ppermute | solution.py:562
  257.9 2.1 fusion.9.refs_0_
  260.0 10.5 %spread.1 = bf16[16,768,128]{2,1,0:T(8,128)(2,1)} custom-call(s32[1]{0:T(128)} %bitcast.18.half_ref.core_ref, bf16[768,768]{1,0:T(8,128)(2,1)} %wkb_ref.1, bf16[768,768]{1,0:T(8,128)(2,1)} %wvb_ref.1, bf16[2,384,2048]{2,1,0:T(8,128)(2,1)} %get-tuple-element.42.a_ref, bf16[768,768]{1,0:T(8,128)(2,1)} %wkb_ref.1, bf16[768,768]{1,0:T(8,128)(2,1)} %wvb_ref.1, ...), custom_call_target="tpu_custom_call" | custom-call | flops 4831838208 | bytes 9437184 | tf_op jit(solution)/shard_map/spread/pallas_call | solution.py:279
  270.5 2.1 reduce_sum.110
  272.6 1.1 collective-permute-start.12
  273.9 2.6 collective-permute-start.14
  276.4 2.1 collective-permute-done.12
  278.5 2.6 collective-permute-done.13
  281.4 0.8 add_convert_fusion.1
  282.2 4.6 %all-to-all-start.3 = ((bf16[16,768,128]{2,1,0:T(8,128)(2,1)}), bf16[16,768,128]{2,1,0:T(8,128)(2,1)}, u32[]{:S(2)}, u32[]{:S(2)}) async-start(bf16[16,768,128]{2,1,0:T(8,128)(2,1)} %spread.1), calls=%async_computation.3 | async-start | bytes 6291456 | tf_op jit(solution)/shard_map/all_to_all | solution.py:630
  286.9 63.7 %all-gather.6.cloned.1.call-done = bf16[3328,384]{1,0:T(8,128)(2,1)} async-done(((bf16[208,384]{1,0:T(8,128)(2,1)}), bf16[3328,384]{1,0:T(8,128)(2,1)}) %all-gather.6.cloned.1.call-update) | async-done | bytes 2555920 | tf_op jit(solution)/shard_map/all_gather | solution.py:619
  350.6 1.4 collective-permute-start.15
  352.0 0.8 fusion.66
  352.8 2.4 convert_reduce_fusion
  355.5 0.6 fusion.15
  356.1 0.9 fusion.32
  357.0 1.1 convert_add_fusion.2
  359.3 0.6 slice_bitcast_fusion.9
  360.5 6.4 %unpack_halves.1 = (f32[768,768]{1,0:T(8,128)}, f32[768,768]{1,0:T(8,128)}, f32[768,768]{1,0:T(8,128)}, f32[768,768]{1,0:T(8,128)}) custom-call(s32[1]{0:T(128)} %bitcast.18.half_ref.core_ref, bf16[16,208,384]{2,1,0:T(8,128)(2,1)} %bitcast.84, bf16[16,208,384]{2,1,0:T(8,128)(2,1)} %collective-permute-done.15.other_ref), custom_call_target="tpu_custom_call" | custom-call | tf_op jit(solution)/shard_map/unpack_halves/pallas_call | solution.py:350
  (105 shorter events, 8.3 us)
Async XLA Ops:
  7.2 83.7 %copy-start = (bf16[768,768]{1,0:T(8,128)(2,1)S(1)}, bf16[768,768]{1,0:T(8,128)(2,1)}, u32[]{:S(2)}) copy-start(bf16[768,768]{1,0:T(8,128)(2,1)} %param.20) | copy-start | bytes 3538948
  7.2 55.0 %all-gather.4.cloned.1.call-start = ((), (), s32[]{:S(2)}) async-start(), calls=%async_computation.4 | async-start | bytes 3342336 | tf_op jit(solution)/shard_map/all_gather | solution.py:501
  8.4 0.5 copy-start.23
  8.9 0.7 copy-start.21
  12.7 5.5 %copy-start.3 = (bf16[768,768]{1,0:T(8,128)(2,1)S(1)}, bf16[768,768]{1,0:T(8,128)(2,1)}, u32[]{:S(2)}) copy-start(bf16[768,768]{1,0:T(8,128)(2,1)} %wq_ref.1) | copy-start | bytes 3538948
  14.2 5.5 %copy-start.9 = (bf16[768,768]{1,0:T(8,128)(2,1)S(1)}, bf16[768,768]{1,0:T(8,128)(2,1)}, u32[]{:S(2)}) copy-start(bf16[768,768]{1,0:T(8,128)(2,1)} %wkb_ref.1) | copy-start | bytes 3538948
  19.7 1.5 copy-start.10
  21.1 1.5 copy-start.20
  21.1 1.5 copy-start.17
  62.2 28.6 %copy-start.2 = (bf16[1,128,768]{2,1,0:T(8,128)(2,1)S(1)}, bf16[1,128,768]{2,1,0:T(8,128)(2,1)}, u32[]{:S(2)}) copy-start(bf16[1,128,768]{2,1,0:T(8,128)(2,1)} %param.14) | copy-start | bytes 589828
  90.8 1.5 copy-start.16
  90.8 2.0 copy-start.7
  116.1 13.5 %all-to-all-start.1 = ((bf16[4,40,1536]{2,1,0:T(8,128)(2,1)}), bf16[4,40,1536]{2,1,0:T(8,128)(2,1)S(1)}, u32[]{:S(2)}, u32[]{:S(2)}) async-start(bf16[4,40,1536]{2,1,0:T(8,128)(2,1)} %bitcast.98), calls=%async_computation.1 | async-start | bytes 983040 | tf_op jit(solution)/shard_map/all_to_all | solution.py:545
  121.0 30.7 %collective-permute-start = (bf16[160,1536]{1,0:T(8,128)(2,1)}, bf16[160,1536]{1,0:T(8,128)(2,1)}, u32[]{:S(2)}, u32[]{:S(2)}) collective-permute-start(bf16[160,1536]{1,0:T(8,128)(2,1)} %bitcast.12.rows_ref.refs_0_.ready_ref), channel_id=1, source_target_pairs={{0,8},{2,10},{4,12},{6,14},{8,16},{10,18},{12,20},{14,22},{16,24},... | collective-permute-start | bytes 1474568 | tf_op jit(solution)/shard_map/ppermute | solution.py:495
  121.5 30.2 %collective-permute-start.1 = (bf16[160,1536]{1,0:T(8,128)(2,1)}, bf16[160,1536]{1,0:T(8,128)(2,1)}, u32[]{:S(2)}, u32[]{:S(2)}) collective-permute-start(bf16[160,1536]{1,0:T(8,128)(2,1)} %bitcast.12.rows_ref.refs_0_.ready_ref), channel_id=1, source_target_pairs={{0,16},{2,18},{4,20},{6,22},{8,24},{10,26},{12,28},{14,30},{16,0},... | collective-permute-start | bytes 1474568 | tf_op jit(solution)/shard_map/ppermute | solution.py:495
  123.9 27.8 %collective-permute-start.2 = (bf16[160,1536]{1,0:T(8,128)(2,1)}, bf16[160,1536]{1,0:T(8,128)(2,1)}, u32[]{:S(2)}, u32[]{:S(2)}) collective-permute-start(bf16[160,1536]{1,0:T(8,128)(2,1)} %bitcast.12.rows_ref.refs_0_.ready_ref), channel_id=1, source_target_pairs={{0,24},{2,26},{4,28},{6,30},{8,0},{10,2},{12,4},{14,6},{16,8},{18,... | collective-permute-start | bytes 1474568 | tf_op jit(solution)/shard_map/ppermute | solution.py:495
  129.9 1.9 copy-start.12
  131.2 1.8 copy-start.5
  133.4 45.9 %collective-permute-start.11 = (bf16[768,384]{1,0:T(8,128)(2,1)S(1)}, bf16[768,384]{1,0:T(8,128)(2,1)S(1)}, u32[]{:S(2)}, u32[]{:S(2)}) collective-permute-start(bf16[768,384]{1,0:T(8,128)(2,1)S(1)} %convolution_convert_fusion.1), channel_id=1, source_target_pairs={{0,32},{32,0},{64,96},{96,64},{1,33},{33,1},{65,97},{97,65},{2,34}... | collective-permute-start | bytes 1769480 | tf_op jit(solution)/shard_map/ppermute | solution.py:585
  134.5 16.0 %copy-start.6 = (f32[128,768]{1,0:T(8,128)S(1)}, f32[128,768]{1,0:T(8,128)}, u32[]{:S(2)}) copy-start(f32[128,768]{1,0:T(8,128)} %get-tuple-element.34.o_ref) | copy-start | bytes 1179652
  150.4 28.8 %collective-permute-start.10 = (bf16[3,768,384]{2,1,0:T(8,128)(2,1)}, bf16[3,768,384]{2,1,0:T(8,128)(2,1)}, u32[]{:S(2)}, u32[]{:S(2)}) collective-permute-start(bf16[3,768,384]{2,1,0:T(8,128)(2,1)} %get-tuple-element.45), channel_id=1, source_target_pairs={{0,32},{32,0},{64,96},{96,64},{1,33},{33,1},{65,97},{97,65},{2,34}... | collective-permute-start | bytes 5308424 | tf_op jit(solution)/shard_map/ppermute | solution.py:591
  160.5 15.9 %copy-start.15 = (f32[3,2,2176]{2,1,0:T(2,128)S(1)}, f32[3,2,2176]{2,1,0:T(2,128)}, u32[]{:S(2)}) copy-start(f32[3,2,2176]{2,1,0:T(2,128)} %get-tuple-element.49) | copy-start | bytes 156676
  160.5 17.3 %copy-start.19 = (f32[1,768]{1,0:T(1,128)S(1)}, f32[1,768]{1,0:T(1,128)}, u32[]{:S(2)}) copy-start(f32[1,768]{1,0:T(1,128)} %get-tuple-element.46) | copy-start | bytes 9220
  160.5 18.0 %copy-start.18 = (bf16[768]{0:T(1024)(128)(2,1)S(1)}, bf16[768]{0:T(1024)(128)(2,1)}, u32[]{:S(2)}) copy-start(bf16[768]{0:T(1024)(128)(2,1)} %param.16) | copy-start | bytes 4612
  179.3 0.8 copy-start.11
  184.6 85.9 %all-to-all-start.2 = ((bf16[16,208,384]{2,1,0:T(8,128)(2,1)}), bf16[16,208,384]{2,1,0:T(8,128)(2,1)}, u32[]{:S(2)}, u32[]{:S(2)}) async-start(bf16[16,208,384]{2,1,0:T(8,128)(2,1)} %merge_halves.1.refs_1_), calls=%async_computation.2 | async-start | bytes 5111808 | tf_op jit(solution)/shard_map/all_to_all | solution.py:606
  189.1 161.5 %all-gather.6.cloned.1.call-start = ((), (), s32[]{:S(2)}) async-start(), calls=%async_computation.5 | async-start | bytes 2715648 | tf_op jit(solution)/shard_map/all_gather | solution.py:619
  190.8 8.2 %collective-permute-start.3 = (bf16[2,96,768]{2,1,0:T(8,128)(2,1)S(1)}, bf16[2,96,768]{2,1,0:T(8,128)(2,1)S(1)}, u32[]{:S(2)}, u32[]{:S(2)}) collective-permute-start(bf16[2,96,768]{2,1,0:T(8,128)(2,1)S(1)} %get-tuple-element.58), channel_id=1, source_target_pairs={{0,1},{1,0},{2,3},{3,2},{4,5},{5,4},{6,7},{7,6},{8,9},{9,8},{10,11... | collective-permute-start | bytes 884744 | tf_op jit(solution)/shard_map/ppermute | solution.py:562
  191.2 38.8 %collective-permute-start.4 = (bf16[2,96,768]{2,1,0:T(8,128)(2,1)S(1)}, bf16[2,96,768]{2,1,0:T(8,128)(2,1)S(1)}, u32[]{:S(2)}, u32[]{:S(2)}) collective-permute-start(bf16[2,96,768]{2,1,0:T(8,128)(2,1)S(1)} %get-tuple-element.64), channel_id=1, source_target_pairs={{0,2},{1,3},{2,4},{3,5},{4,6},{5,7},{6,0},{7,1},{8,10},{9,11},{10,... | collective-permute-start | bytes 884744 | tf_op jit(solution)/shard_map/ppermute | solution.py:562
  192.4 46.8 %collective-permute-start.5 = (bf16[2,96,768]{2,1,0:T(8,128)(2,1)S(1)}, bf16[2,96,768]{2,1,0:T(8,128)(2,1)S(1)}, u32[]{:S(2)}, u32[]{:S(2)}) collective-permute-start(bf16[2,96,768]{2,1,0:T(8,128)(2,1)S(1)} %get-tuple-element.63), channel_id=1, source_target_pairs={{0,3},{1,2},{2,5},{3,4},{4,7},{5,6},{6,1},{7,0},{8,11},{9,10},{10,... | collective-permute-start | bytes 884744 | tf_op jit(solution)/shard_map/ppermute | solution.py:562
  194.4 55.8 %collective-permute-start.6 = (bf16[2,96,768]{2,1,0:T(8,128)(2,1)S(1)}, bf16[2,96,768]{2,1,0:T(8,128)(2,1)S(1)}, u32[]{:S(2)}, u32[]{:S(2)}) collective-permute-start(bf16[2,96,768]{2,1,0:T(8,128)(2,1)S(1)} %get-tuple-element.62), channel_id=1, source_target_pairs={{0,4},{1,5},{2,6},{3,7},{4,0},{5,1},{6,2},{7,3},{8,12},{9,13},{10,... | collective-permute-start | bytes 884744 | tf_op jit(solution)/shard_map/ppermute | solution.py:562
  195.9 62.0 %collective-permute-start.7 = (bf16[2,96,768]{2,1,0:T(8,128)(2,1)S(1)}, bf16[2,96,768]{2,1,0:T(8,128)(2,1)S(1)}, u32[]{:S(2)}, u32[]{:S(2)}) collective-permute-start(bf16[2,96,768]{2,1,0:T(8,128)(2,1)S(1)} %get-tuple-element.61), channel_id=1, source_target_pairs={{0,5},{1,4},{2,7},{3,6},{4,1},{5,0},{6,3},{7,2},{8,13},{9,12},{10,... | collective-permute-start | bytes 884744 | tf_op jit(solution)/shard_map/ppermute | solution.py:562
  199.0 58.9 %collective-permute-start.8 = (bf16[2,96,768]{2,1,0:T(8,128)(2,1)S(1)}, bf16[2,96,768]{2,1,0:T(8,128)(2,1)S(1)}, u32[]{:S(2)}, u32[]{:S(2)}) collective-permute-start(bf16[2,96,768]{2,1,0:T(8,128)(2,1)S(1)} %get-tuple-element.60), channel_id=1, source_target_pairs={{0,6},{1,7},{2,0},{3,1},{4,2},{5,3},{6,4},{7,5},{8,14},{9,15},{10,... | collective-permute-start | bytes 884744 | tf_op jit(solution)/shard_map/ppermute | solution.py:562
  230.1 27.8 %collective-permute-start.9 = (bf16[2,96,768]{2,1,0:T(8,128)(2,1)S(1)}, bf16[2,96,768]{2,1,0:T(8,128)(2,1)S(1)}, u32[]{:S(2)}, u32[]{:S(2)}) collective-permute-start(bf16[2,96,768]{2,1,0:T(8,128)(2,1)S(1)} %get-tuple-element.59), channel_id=1, source_target_pairs={{0,7},{1,6},{2,1},{3,0},{4,3},{5,2},{6,5},{7,4},{8,15},{9,14},{10,... | collective-permute-start | bytes 884744 | tf_op jit(solution)/shard_map/ppermute | solution.py:562
  272.6 5.9 %collective-permute-start.12 = (bf16[208,384]{1,0:T(8,128)(2,1)S(1)}, bf16[208,384]{1,0:T(8,128)(2,1)S(1)}, u32[]{:S(2)}, u32[]{:S(2)}) collective-permute-start(bf16[208,384]{1,0:T(8,128)(2,1)S(1)} %reduce_sum.110), channel_id=1, source_target_pairs={{0,1},{1,64},{32,33},{33,96},{64,65},{65,0},{96,97},{97,32},{2,3},... | collective-permute-start | bytes 479240 | tf_op jit(solution)/shard_map/ppermute | solution.py:618
  273.7 7.3 %collective-permute-start.13 = (bf16[208,384]{1,0:T(8,128)(2,1)S(1)}, bf16[208,384]{1,0:T(8,128)(2,1)S(1)}, u32[]{:S(2)}, u32[]{:S(2)}) collective-permute-start(bf16[208,384]{1,0:T(8,128)(2,1)S(1)} %reduce_sum.110), channel_id=1, source_target_pairs={{0,64},{1,65},{32,96},{33,97},{64,0},{65,1},{96,32},{97,33},{2,66}... | collective-permute-start | bytes 479240 | tf_op jit(solution)/shard_map/ppermute | solution.py:618
  273.9 7.6 %collective-permute-start.14 = (bf16[208,384]{1,0:T(8,128)(2,1)S(1)}, bf16[208,384]{1,0:T(8,128)(2,1)S(1)}, u32[]{:S(2)}, u32[]{:S(2)}) collective-permute-start(bf16[208,384]{1,0:T(8,128)(2,1)S(1)} %reduce_sum.110), channel_id=1, source_target_pairs={{0,65},{1,0},{32,97},{33,32},{64,1},{65,64},{96,33},{97,96},{2,67}... | collective-permute-start | bytes 479240 | tf_op jit(solution)/shard_map/ppermute | solution.py:618
  282.2 69.7 %copy-start.13 = (bf16[128,384]{1,0:T(8,128)(2,1)S(1)}, bf16[128,384]{1,0:T(8,128)(2,1)}, u32[]{:S(2)}) copy-start(bf16[128,384]{1,0:T(8,128)(2,1)} %get-tuple-element.41) | copy-start | bytes 294916
  282.2 69.7 %copy-start.14 = (bf16[128,384]{1,0:T(8,128)(2,1)S(1)}, bf16[128,384]{1,0:T(8,128)(2,1)}, u32[]{:S(2)}) copy-start(bf16[128,384]{1,0:T(8,128)(2,1)} %get-tuple-element.40) | copy-start | bytes 294916
  282.2 69.7 %copy-start.8 = (f32[2,96,768]{2,1,0:T(8,128)S(1)}, f32[2,96,768]{2,1,0:T(8,128)}, u32[]{:S(2)}) copy-start(f32[2,96,768]{2,1,0:T(8,128)} %fusion.9.refs_0_) | copy-start | bytes 1769476
  282.2 70.6 %all-to-all-start.3 = ((bf16[16,768,128]{2,1,0:T(8,128)(2,1)}), bf16[16,768,128]{2,1,0:T(8,128)(2,1)}, u32[]{:S(2)}, u32[]{:S(2)}) async-start(bf16[16,768,128]{2,1,0:T(8,128)(2,1)} %spread.1), calls=%async_computation.3 | async-start | bytes 6291456 | tf_op jit(solution)/shard_map/all_to_all | solution.py:630
  350.6 6.5 %collective-permute-start.15 = (bf16[16,208,384]{2,1,0:T(8,128)(2,1)}, bf16[16,208,384]{2,1,0:T(8,128)(2,1)}, u32[]{:S(2)}, u32[]{:S(2)}) collective-permute-start(bf16[16,208,384]{2,1,0:T(8,128)(2,1)} %bitcast.82), channel_id=1, source_target_pairs={{0,32},{32,0},{64,96},{96,64},{1,33},{33,1},{65,97},{97,65},{2,34}... | collective-permute-start | bytes 7667720 | tf_op jit(solution)/shard_map/ppermute | solution.py:620
  352.8 2.6 copy-start.4
  355.3 0.8 copy-start.24
  355.3 0.9 copy-start.22
  359.9 7.0 %copy-start.1 = (bf16[768,768]{1,0:T(8,128)(2,1)S(1)}, bf16[768,768]{1,0:T(8,128)(2,1)}, u32[]{:S(2)}) copy-start(bf16[768,768]{1,0:T(8,128)(2,1)} %param.20) | copy-start | bytes 3538948
Sparse Core Ops, SparseCore 0:
  11.4 50.7 all-gather.3
  282.3 68.1 all-gather.5

commit v2 on v1

--- a/solution.py
+++ b/solution.py
@@ -428,7 +428,7 @@
     for d in range(2):
         to = lax.rem(d + place_ref[1], 2)
         for i in range(2):
-            out_ref[0, to, i] = found[i][d * share : (d + 1) * share]
+            out_ref[to, 0, i] = found[i][d * share : (d + 1) * share]
 
 
 def expert_grads(place, parts, w_in_t, w_out, side):
@@ -443,12 +443,12 @@
             grid=(side,),
             in_specs=[pl.BlockSpec(part.shape, lambda c, place: (0, 0)) for part in parts] + [weight, weight],
             out_specs=pl.BlockSpec(
-                (1, 2, 2, chunk // 2, width),
-                lambda c, place: (lax.rem(c + side - place[0], side), 0, 0, 0, 0),
+                (2, 1, 2, chunk // 2, width),
+                lambda c, place: (0, lax.rem(c + side - place[0], side), 0, 0, 0),
             ),
             scratch_shapes=[pltpu.VMEM((count, 2 * width), BF16)],
         ),
-        out_shape=jax.ShapeDtypeStruct((side, 2, 2, chunk // 2, width), BF16),
+        out_shape=jax.ShapeDtypeStruct((2, side, 2, chunk // 2, width), BF16),
         compiler_params=pltpu.CompilerParams(vmem_limit_bytes=56 * MIB),
         cost_estimate=pl.CostEstimate(
             flops=8 * count * width * units, bytes_accessed=8 * width * units, transcendentals=count * units
@@ -549,21 +549,6 @@
 
     parts = [arrived] + [ring(arrived, True, step) for step in range(1, side)]
     shares = expert_grads(jnp.stack([ctx_x, dp]).astype(jnp.int32), parts, w_in_slice, w_out_slice, side)
-    expert_sum = shares[0, 0].astype(F32)
-    for step in range(side):
-        for flip in range(2):
-            if step == 0 and flip == 0:
-                continue
-            route_pairs = []
-            for c in range(ctx_count):
-                to = c // side * side + (c % side + step) % side
-                for d in range(2):
-                    route_pairs.append((c * 2 + d, to * 2 + (d ^ flip)))
-            moved = lax.ppermute(shares[step, flip], ("context", "dp"), route_pairs)
-            expert_sum = expert_sum + moved.astype(F32)
-    grad_w_in_out = expert_sum[0].T[None]
-    grad_w_out_out = expert_sum[1][None]
-
     grad_gate = jnp.sum(grad_out * picked, axis=-1)
     grad_logits = (grad_gate * gate)[:, None] * (chosen_f - router_probs)
     grad_router = lax.dot_general(grad_logits, normed2, (((0,), (0,)), ((), ())), precision=HIGHEST)
@@ -602,6 +587,14 @@
     )
     small = jnp.pad(small, (0, ctx_count * 16 * cols - small.size)).astype(BF16)
     merged = merge_halves(grads_b, other, both_out[1], other_out, small.reshape(ctx_count, 16, cols))
+    shares, merged = lax.optimization_barrier((shares, merged))
+    other = lax.ppermute(shares[1], "dp", [(0, 1), (1, 0)])
+    paired = (shares[0].astype(F32) + other.astype(F32)).astype(BF16)
+    expert_sum = paired[0].astype(F32)
+    for step in range(1, side):
+        expert_sum = expert_sum + ring(paired[step], False, step).astype(F32)
+    grad_w_in_out = expert_sum[0].T[None]
+    grad_w_out_out = expert_sum[1][None]
     part = spread(core, w_key, w_value, terms_b, terms_a, tok_count, (expert_sum, merged))
     merged = lax.all_to_all(merged, "context", split_axis=0, concat_axis=0, tiled=True)
     merged = jnp.sum(merged.astype(F32), axis=0).astype(BF16)

time: 375 us -> 355 us (0.947)
  waiting for transfers between devices: 166 us -> 156 us
  starting transfers between devices: 35.6 us -> 27.8 us
    ppermute x7 -> x1, waiting for transfers between devices: 55.1 us -> 22.3 us  [per_device(): other = lax.ppermute(shares[1], 'dp', [(0, 1), (1, 0)])]
    ppermute x3 -> x6, waiting for transfers between devices: 0.01 us -> 21.3 us  [ring(): return lax.ppermute(values, 'context', pairs)]
    ppermute x7 -> x1, starting transfers between devices: 12 us -> 0.45 us  [per_device(): other = lax.ppermute(shares[1], 'dp', [(0, 1), (1, 0)])]
  transfers between devices with their start and end apart: 21 -> 18, of which waited for: 11 -> 9; matrix products, arithmetic and copies ran while one was open for 8% -> 8% of each run, Pallas kernels for 14% -> 14%
where the time goes in v2:
time: 355 us; the launch traced here: 354 us
  waiting for transfers between devices  156 us (44%)
  Pallas kernels  99.7 us (28%)
  starting transfers between devices  27.8 us (8%)
  local copies, waits for them, and re-layouts  17.8 us (5%)
  other arithmetic  17 us (5%)
  between operations  14.6 us (4%)
  blocking collectives  14.3 us (4%)
  matrix products  7.12 us (2%)
    all_gather x1, waiting for transfers between devices, per_device(): whole = lax.all_gather(total.astype(BF16), 'context', axis=0)  62.6 us
    all_gather x1, waiting for transfers between devices, per_device(): act_all = lax.all_gather(act, 'context', axis=0, tiled=True)  37.9 us
    pallas_call x2, Pallas kernels, attend_back(): pl.pallas_call(attend_back_kernel, grid_spec=pltpu.PrefetchScalarGridSpec...  31.8 us
    pallas_call x1, Pallas kernels, attend(): pl.pallas_call(attend_kernel, grid=(pairs,), in_specs=[whole(length), who...  28.6 us
    ppermute x1, waiting for transfers between devices, per_device(): other = lax.ppermute(shares[1], 'dp', [(0, 1), (1, 0)])  22.3 us
    ppermute x6, waiting for transfers between devices, ring(): return lax.ppermute(values, 'context', pairs)  21.3 us
    all_to_all x1, blocking collectives, per_device(): lax.all_to_all(going, 'expert', split_axis=0, concat_axis=0, tiled=True)  14.3 us
    pallas_call x1, Pallas kernels, spread(): pl.pallas_call(spread_kernel, grid_spec=pltpu.PrefetchScalarGridSpec(num_...  10.6 us
  transfers between devices with their start and end apart: 18, of which 9 were waited for; matrix products, arithmetic and copies ran while one was open for 8% of the time, Pallas kernels for 14%

profile of v2, /device:TPU:1, one launch (start us, length us, event | category | flops | bytes accessed | tf_op | source)
XLA Modules:
  0.0 354.3 jit_solution(13606881059153404400)
XLA Ops:
  7.2 1.1 fusion.9
  8.4 0.7 convert_element_type.132
  9.1 1.7 fusion.11.own_ref
  10.8 1.4 constant_dynamic-slice_fusion
  12.2 1.5 copy.38
  13.9 0.7 reshape.142.win_ref
  14.6 2.4 copy.39
  17.1 1.5 copy.40
  18.5 2.4 copy.41
  21.4 2.4 dynamic-slice_bitcast_fusion.refs_1_.refs_5_
  23.8 37.9 %all-gather.4.cloned.1.call-done.act_ref = bf16[2048,768]{1,0:T(8,128)(2,1)} async-done(((bf16[128,768]{1,0:T(8,128)(2,1)}), bf16[2048,768]{1,0:T(8,128)(2,1)}) %all-gather.4.cloned.1.call-update) | async-done | bytes 3145744 | tf_op jit(solution)/shard_map/all_gather | solution.py:501
  61.7 28.6 %attend.1 = (bf16[128,768]{1,0:T(8,128)(2,1)}, bf16[2048,768]{1,0:T(8,128)(2,1)}, bf16[2048,768]{1,0:T(8,128)(2,1)}, f32[128,768]{1,0:T(8,128)}, f32[128,768]{1,0:T(8,128)}, /*index=5*/bf16[6,256,2048]{2,1,0:T(8,128)(2,1)}) custom-call(bf16[2048,768]{1,0:T(8,128)(2,1)} %all-gather.4.cloned.1.call-done.act_ref, bf16[128,768]{1,0:T(8,128)(2,1)} %fusion.11.own_ref, ...), custom_call_target="tpu_custom_call" | custom-call | flops 6442450944 | bytes 25165824 | tf_op jit(solution)/shard_map/attend/pallas_call | solution.py:120
  90.3 1.5 multiply_reduce_fusion.2
  92.7 14.3 %all_to_all.20 = bf16[4,40,1536]{2,1,0:T(8,128)(2,1)} all-to-all(bf16[4,40,1536]{2,1,0:T(8,128)(2,1)S(1)} %bitcast.83), channel_id=1, replica_groups=mesh['expert'=4,'context'=16,'dp'=2] {'expert'}, dimensions={0} | all-to-all | bytes 983040 | tf_op jit(solution)/shard_map/all_to_all | solution.py:541
  107.1 9.0 %expert_both.1 = bf16[160,1536]{1,0:T(8,128)(2,1)} custom-call(bf16[160,1536]{1,0:T(8,128)(2,1)} %bitcast.95, bf16[768,3072]{1,0:T(8,128)(2,1)} %bitcast.102, bf16[3072,768]{1,0:T(8,128)(2,1)} %bitcast.103), custom_call_target="tpu_custom_call" | custom-call | flops 3019898880 | bytes 9437184 | tf_op jit(solution)/shard_map/expert_both/pallas_call | solution.py:393
  116.1 4.4 %all-to-all-start.1 = ((bf16[4,40,1536]{2,1,0:T(8,128)(2,1)}), bf16[4,40,1536]{2,1,0:T(8,128)(2,1)S(1)}, u32[]{:S(2)}, u32[]{:S(2)}) async-start(bf16[4,40,1536]{2,1,0:T(8,128)(2,1)} %bitcast.101), calls=%async_computation.1 | async-start | bytes 983040 | tf_op jit(solution)/shard_map/all_to_all | solution.py:545
  120.5 0.6 pad_add_fusion.place_ref
  121.1 0.5 collective-permute-start
  121.5 2.4 collective-permute-start.1
  123.9 0.8 collective-permute-start.2
  124.7 4.9 %all-to-all-done.1 = bf16[4,40,1536]{2,1,0:T(8,128)(2,1)S(1)} async-done(((bf16[4,40,1536]{2,1,0:T(8,128)(2,1)}), bf16[4,40,1536]{2,1,0:T(8,128)(2,1)S(1)}, u32[]{:S(2)}, u32[]{:S(2)}) %all-to-all-start.1) | async-done | bytes 491552 | tf_op jit(solution)/shard_map/all_to_all | solution.py:545
  129.9 0.8 fusion.8
  130.7 0.5 multiply_reduce_fusion
  131.9 1.2 fusion.4.do_ref
  133.4 1.1 collective-permute-start.4
  134.6 15.9 %attend_back.3 = (bf16[128,384]{1,0:T(8,128)(2,1)}, bf16[2,384,2048]{2,1,0:T(8,128)(2,1)}, bf16[3,768,384]{2,1,0:T(8,128)(2,1)}, f32[1,768]{1,0:T(1,128)}, f32[3,2,2176]{2,1,0:T(2,128)}) custom-call(s32[1]{0:T(128)S(6)} %sub.41.half_ref, bf16[6,256,2048]{2,1,0:T(8,128)(2,1)} %get-tuple-element.37.p_ref, bf16[128,768]{1,0:T(8,128)(2,1)} %fusion.4.do_ref, ...), custom_call_target="tpu_custom_call" | custom-call | flops 6442450944 | bytes 14155776 | tf_op jit(solution)/shard_map/attend_back/pallas_call | solution.py:221
  150.6 1.2 convolution_convert_fusion.2.mine_out_ref
  151.8 8.8 %expert_grads.1.ready_ref = bf16[2,4,2,96,768]{4,3,2,1,0:T(8,128)(2,1)} custom-call(s32[2]{0:T(128)} %pad_add_fusion.place_ref, bf16[160,1536]{1,0:T(8,128)(2,1)} %bitcast.97, bf16[160,1536]{1,0:T(8,128)(2,1)} %collective-permute-done.refs_1_, bf16[160,1536]{1,0:T(8,128)(2,1)} %collective-permute-done.1.refs_2_, ...), custom_call_target="tpu_custom_call" | custom-call | flops 3019898880 | bytes 4718592 | tf_op jit(solution)/shard_map/expert_grads/pallas_call | solution.py:439
  160.6 15.9 %attend_back.2 = (bf16[128,384]{1,0:T(8,128)(2,1)}, bf16[2,384,2048]{2,1,0:T(8,128)(2,1)}, bf16[3,768,384]{2,1,0:T(8,128)(2,1)}, f32[1,768]{1,0:T(1,128)}, f32[3,2,2176]{2,1,0:T(2,128)}) custom-call(s32[1]{0:T(128)} %bitcast.18.half_ref.core_ref, bf16[6,256,2048]{2,1,0:T(8,128)(2,1)} %get-tuple-element.37.p_ref, bf16[128,768]{1,0:T(8,128)(2,1)} %fusion.4.do_ref, ...), custom_call_target="tpu_custom_call" | custom-call | flops 6442450944 | bytes 14155776 | tf_op jit(solution)/shard_map/attend_back/pallas_call | solution.py:221
  176.5 0.8 broadcast_select_fusion.3
  177.8 0.7 add_reduce_fusion
  178.6 0.8 reshape.150.small_ref
  179.3 0.8 copy-done.10
  180.1 4.7 %merge_halves.1.refs_1_ = bf16[16,208,384]{2,1,0:T(8,128)(2,1)} custom-call(bf16[3,768,384]{2,1,0:T(8,128)(2,1)} %get-tuple-element.46.mine_ref, bf16[3,768,384]{2,1,0:T(8,128)(2,1)} %collective-permute-done.3.other_ref, bf16[768,384]{1,0:T(8,128)(2,1)} %convolution_convert_fusion.2.mine_out_ref, bf16[768,384]{1,0:T(8,128)(2,1)} %copy-done.10, ...), custom_call_target="tpu_custom_call" | custom-call | tf_op jit(solution)/shard_map/merge_halves/pallas_call | solution.py:318
  184.9 0.5 collective-permute-start.5
  185.4 4.5 %all-to-all-start.2 = ((bf16[16,208,384]{2,1,0:T(8,128)(2,1)}), bf16[16,208,384]{2,1,0:T(8,128)(2,1)}, u32[]{:S(2)}, u32[]{:S(2)}) async-start(bf16[16,208,384]{2,1,0:T(8,128)(2,1)} %merge_halves.1.refs_1_), calls=%async_computation.2 | async-start | bytes 5111808 | tf_op jit(solution)/shard_map/all_to_all | solution.py:599
  189.9 22.3 %collective-permute-done.5 = bf16[4,2,96,768]{3,2,1,0:T(8,128)(2,1)S(1)} collective-permute-done((bf16[4,2,96,768]{3,2,1,0:T(8,128)(2,1)S(1)}, bf16[4,2,96,768]{3,2,1,0:T(8,128)(2,1)S(1)}, u32[]{:S(2)}, u32[]{:S(2)}) %collective-permute-start.5) | collective-permute-done | bytes 1179680 | tf_op jit(solution)/shard_map/ppermute | solution.py:591
  212.2 1.5 fusion
  213.8 0.5 collective-permute-start.6
  214.3 2.4 collective-permute-start.7
  216.7 0.8 collective-permute-start.8
  217.5 13.2 %collective-permute-done.6 = bf16[2,96,768]{2,1,0:T(8,128)(2,1)S(1)} collective-permute-done((bf16[2,96,768]{2,1,0:T(8,128)(2,1)S(1)}, bf16[2,96,768]{2,1,0:T(8,128)(2,1)S(1)}, u32[]{:S(2)}, u32[]{:S(2)}) %collective-permute-start.6) | collective-permute-done | bytes 294944 | tf_op jit(solution)/shard_map/ppermute | solution.py:495
  230.7 8.2 %collective-permute-done.7 = bf16[2,96,768]{2,1,0:T(8,128)(2,1)S(1)} collective-permute-done((bf16[2,96,768]{2,1,0:T(8,128)(2,1)S(1)}, bf16[2,96,768]{2,1,0:T(8,128)(2,1)S(1)}, u32[]{:S(2)}, u32[]{:S(2)}) %collective-permute-start.7) | collective-permute-done | bytes 294944 | tf_op jit(solution)/shard_map/ppermute | solution.py:495
  238.9 1.0 fusion.6.refs_0_
  239.8 10.6 %spread.1 = bf16[16,768,128]{2,1,0:T(8,128)(2,1)} custom-call(s32[1]{0:T(128)} %bitcast.18.half_ref.core_ref, bf16[768,768]{1,0:T(8,128)(2,1)} %wkb_ref.1, bf16[768,768]{1,0:T(8,128)(2,1)} %wvb_ref.1, bf16[2,384,2048]{2,1,0:T(8,128)(2,1)} %get-tuple-element.44.a_ref, bf16[768,768]{1,0:T(8,128)(2,1)} %wkb_ref.1, bf16[768,768]{1,0:T(8,128)(2,1)} %wvb_ref.1, ...), custom_call_target="tpu_custom_call" | custom-call | flops 4831838208 | bytes 9437184 | tf_op jit(solution)/shard_map/spread/pallas_call | solution.py:279
  250.4 2.1 reduce_sum.110
  252.5 0.8 collective-permute-start.10
  253.3 2.8 collective-permute-start.11
  256.1 2.1 collective-permute-done.10
  258.2 1.9 collective-permute-done.11
  260.1 2.9 collective-permute-done.9
  262.9 0.8 add_convert_fusion.1
  263.7 4.8 %all-to-all-start.3 = ((bf16[16,768,128]{2,1,0:T(8,128)(2,1)}), bf16[16,768,128]{2,1,0:T(8,128)(2,1)}, u32[]{:S(2)}, u32[]{:S(2)}) async-start(bf16[16,768,128]{2,1,0:T(8,128)(2,1)} %spread.1), calls=%async_computation.3 | async-start | bytes 6291456 | tf_op jit(solution)/shard_map/all_to_all | solution.py:623
  268.6 62.6 %all-gather.6.cloned.1.call-done = bf16[3328,384]{1,0:T(8,128)(2,1)} async-done(((bf16[208,384]{1,0:T(8,128)(2,1)}), bf16[3328,384]{1,0:T(8,128)(2,1)}) %all-gather.6.cloned.1.call-update) | async-done | bytes 2555920 | tf_op jit(solution)/shard_map/all_gather | solution.py:612
  331.2 1.4 collective-permute-start.12
  332.6 0.8 fusion.63
  333.4 2.4 convert_reduce_fusion
  336.1 0.6 fusion.12
  336.8 0.9 fusion.29
  337.7 1.1 convert_add_fusion.3
  339.3 0.6 slice_bitcast_fusion.7
  339.9 0.6 slice_bitcast_fusion.6
  340.5 0.6 fusion.64
  341.1 6.4 %unpack_halves.1 = (f32[768,768]{1,0:T(8,128)}, f32[768,768]{1,0:T(8,128)}, f32[768,768]{1,0:T(8,128)}, f32[768,768]{1,0:T(8,128)}) custom-call(s32[1]{0:T(128)} %bitcast.18.half_ref.core_ref, bf16[16,208,384]{2,1,0:T(8,128)(2,1)} %bitcast.81, bf16[16,208,384]{2,1,0:T(8,128)(2,1)} %collective-permute-done.12.other_ref), custom_call_target="tpu_custom_call" | custom-call | tf_op jit(solution)/shard_map/unpack_halves/pallas_call | solution.py:350
  (105 shorter events, 4.5 us)
Async XLA Ops:
  7.2 83.2 %copy-start = (bf16[768,768]{1,0:T(8,128)(2,1)S(1)}, bf16[768,768]{1,0:T(8,128)(2,1)}, u32[]{:S(2)}) copy-start(bf16[768,768]{1,0:T(8,128)(2,1)} %param.20) | copy-start | bytes 3538948
  7.2 54.5 %all-gather.4.cloned.1.call-start = ((), (), s32[]{:S(2)}) async-start(), calls=%async_computation.4 | async-start | bytes 3342336 | tf_op jit(solution)/shard_map/all_gather | solution.py:501
  8.4 5.3 %copy-start.25 = (f32[128]{0:T(128)}, f32[128]{0:T(128)S(1)}, u32[]{:S(2)}) copy-start(f32[128]{0:T(128)S(1)} %fusion.9) | copy-start | bytes 1540
  12.2 1.5 copy-start.17
  12.2 1.6 copy-start.20
  13.7 3.4 copy-start.9
  18.5 2.4 copy-start.22
  18.5 2.4 copy-start.18
  61.7 28.6 %copy-start.2 = (bf16[1,128,768]{2,1,0:T(8,128)(2,1)S(1)}, bf16[1,128,768]{2,1,0:T(8,128)(2,1)}, u32[]{:S(2)}) copy-start(bf16[1,128,768]{2,1,0:T(8,128)(2,1)} %param.14) | copy-start | bytes 589828
  90.3 1.5 copy-start.16
  90.3 2.0 copy-start.6
  107.1 14.0 %copy-start.11 = (bf16[4,40,1536]{2,1,0:T(8,128)(2,1)S(1)}, bf16[4,40,1536]{2,1,0:T(8,128)(2,1)}, u32[]{:S(2)}) copy-start(bf16[4,40,1536]{2,1,0:T(8,128)(2,1)} %all_to_all.20) | copy-start | bytes 1474564
  116.1 13.5 %all-to-all-start.1 = ((bf16[4,40,1536]{2,1,0:T(8,128)(2,1)}), bf16[4,40,1536]{2,1,0:T(8,128)(2,1)S(1)}, u32[]{:S(2)}, u32[]{:S(2)}) async-start(bf16[4,40,1536]{2,1,0:T(8,128)(2,1)} %bitcast.101), calls=%async_computation.1 | async-start | bytes 983040 | tf_op jit(solution)/shard_map/all_to_all | solution.py:545
  121.1 30.7 %collective-permute-start = (bf16[160,1536]{1,0:T(8,128)(2,1)S(1)}, bf16[160,1536]{1,0:T(8,128)(2,1)}, u32[]{:S(2)}, u32[]{:S(2)}) collective-permute-start(bf16[160,1536]{1,0:T(8,128)(2,1)S(1)} %bitcast.98), channel_id=1, source_target_pairs={{0,8},{2,10},{4,12},{6,14},{8,16},{10,18},{12,20},{14,22},{16,24},... | collective-permute-start | bytes 1474568 | tf_op jit(solution)/shard_map/ppermute | solution.py:495
  121.5 30.2 %collective-permute-start.1 = (bf16[160,1536]{1,0:T(8,128)(2,1)S(1)}, bf16[160,1536]{1,0:T(8,128)(2,1)}, u32[]{:S(2)}, u32[]{:S(2)}) collective-permute-start(bf16[160,1536]{1,0:T(8,128)(2,1)S(1)} %bitcast.99), channel_id=1, source_target_pairs={{0,16},{2,18},{4,20},{6,22},{8,24},{10,26},{12,28},{14,30},{16,0},... | collective-permute-start | bytes 1474568 | tf_op jit(solution)/shard_map/ppermute | solution.py:495
  123.9 27.8 %collective-permute-start.2 = (bf16[160,1536]{1,0:T(8,128)(2,1)S(1)}, bf16[160,1536]{1,0:T(8,128)(2,1)}, u32[]{:S(2)}, u32[]{:S(2)}) collective-permute-start(bf16[160,1536]{1,0:T(8,128)(2,1)S(1)} %bitcast.100), channel_id=1, source_target_pairs={{0,24},{2,26},{4,28},{6,30},{8,0},{10,2},{12,4},{14,6},{16,8},{18,... | collective-permute-start | bytes 1474568 | tf_op jit(solution)/shard_map/ppermute | solution.py:495
  130.7 1.1 copy-start.12
  131.7 1.4 copy-start.23
  131.7 1.4 copy-start.4
  133.4 45.9 %collective-permute-start.4 = (bf16[768,384]{1,0:T(8,128)(2,1)S(1)}, bf16[768,384]{1,0:T(8,128)(2,1)S(1)}, u32[]{:S(2)}, u32[]{:S(2)}) collective-permute-start(bf16[768,384]{1,0:T(8,128)(2,1)S(1)} %convolution_convert_fusion.1), channel_id=1, source_target_pairs={{0,32},{32,0},{64,96},{96,64},{1,33},{33,1},{65,97},{97,65},{2,34}... | collective-permute-start | bytes 1769480 | tf_op jit(solution)/shard_map/ppermute | solution.py:570
  134.6 16.0 %copy-start.5 = (f32[128,768]{1,0:T(8,128)S(1)}, f32[128,768]{1,0:T(8,128)}, u32[]{:S(2)}) copy-start(f32[128,768]{1,0:T(8,128)} %get-tuple-element.36.o_ref) | copy-start | bytes 1179652
  150.5 28.9 %collective-permute-start.3 = (bf16[3,768,384]{2,1,0:T(8,128)(2,1)}, bf16[3,768,384]{2,1,0:T(8,128)(2,1)}, u32[]{:S(2)}, u32[]{:S(2)}) collective-permute-start(bf16[3,768,384]{2,1,0:T(8,128)(2,1)} %get-tuple-element.47), channel_id=1, source_target_pairs={{0,32},{32,0},{64,96},{96,64},{1,33},{33,1},{65,97},{97,65},{2,34}... | collective-permute-start | bytes 5308424 | tf_op jit(solution)/shard_map/ppermute | solution.py:576
  160.5 15.9 %copy-start.15 = (f32[3,2,2176]{2,1,0:T(2,128)S(1)}, f32[3,2,2176]{2,1,0:T(2,128)}, u32[]{:S(2)}) copy-start(f32[3,2,2176]{2,1,0:T(2,128)} %get-tuple-element.51) | copy-start | bytes 156676
  160.5 17.3 %copy-start.21 = (f32[1,768]{1,0:T(1,128)S(1)}, f32[1,768]{1,0:T(1,128)}, u32[]{:S(2)}) copy-start(f32[1,768]{1,0:T(1,128)} %get-tuple-element.48) | copy-start | bytes 9220
  160.5 18.0 %copy-start.19 = (bf16[768]{0:T(1024)(128)(2,1)S(1)}, bf16[768]{0:T(1024)(128)(2,1)}, u32[]{:S(2)}) copy-start(bf16[768]{0:T(1024)(128)(2,1)} %param.16) | copy-start | bytes 4612
  179.3 0.8 copy-start.10
  180.1 4.7 %copy-start.7 = (bf16[2,4,2,96,768]{4,3,2,1,0:T(8,128)(2,1)S(1)}, bf16[2,4,2,96,768]{4,3,2,1,0:T(8,128)(2,1)}, u32[]{:S(2)}) copy-start(bf16[2,4,2,96,768]{4,3,2,1,0:T(8,128)(2,1)} %expert_grads.1.ready_ref) | copy-start | bytes 7077892
  184.9 27.3 %collective-permute-start.5 = (bf16[4,2,96,768]{3,2,1,0:T(8,128)(2,1)S(1)}, bf16[4,2,96,768]{3,2,1,0:T(8,128)(2,1)S(1)}, u32[]{:S(2)}, u32[]{:S(2)}) collective-permute-start(bf16[4,2,96,768]{3,2,1,0:T(8,128)(2,1)S(1)} %slice_bitcast_fusion), channel_id=1, source_target_pairs={{0,1},{1,0},{2,3},{3,2},{4,5},{5,4},{6,7},{7,6},{8,9},{9,8},{10,11... | collective-permute-start | bytes 3538952 | tf_op jit(solution)/shard_map/ppermute | solution.py:591
  185.4 65.0 %all-to-all-start.2 = ((bf16[16,208,384]{2,1,0:T(8,128)(2,1)}), bf16[16,208,384]{2,1,0:T(8,128)(2,1)}, u32[]{:S(2)}, u32[]{:S(2)}) async-start(bf16[16,208,384]{2,1,0:T(8,128)(2,1)} %merge_halves.1.refs_1_), calls=%async_computation.2 | async-start | bytes 5111808 | tf_op jit(solution)/shard_map/all_to_all | solution.py:599
  189.8 141.4 %all-gather.6.cloned.1.call-start = ((), (), s32[]{:S(2)}) async-start(), calls=%async_computation.5 | async-start | bytes 2715648 | tf_op jit(solution)/shard_map/all_gather | solution.py:612
  213.8 16.9 %collective-permute-start.6 = (bf16[2,96,768]{2,1,0:T(8,128)(2,1)S(1)}, bf16[2,96,768]{2,1,0:T(8,128)(2,1)S(1)}, u32[]{:S(2)}, u32[]{:S(2)}) collective-permute-start(bf16[2,96,768]{2,1,0:T(8,128)(2,1)S(1)} %get-tuple-element.62), channel_id=1, source_target_pairs={{0,2},{2,4},{4,6},{6,0},{8,10},{10,12},{12,14},{14,8},{16,18},{18,... | collective-permute-start | bytes 884744 | tf_op jit(solution)/shard_map/ppermute | solution.py:495
  214.3 24.5 %collective-permute-start.7 = (bf16[2,96,768]{2,1,0:T(8,128)(2,1)S(1)}, bf16[2,96,768]{2,1,0:T(8,128)(2,1)S(1)}, u32[]{:S(2)}, u32[]{:S(2)}) collective-permute-start(bf16[2,96,768]{2,1,0:T(8,128)(2,1)S(1)} %get-tuple-element.64), channel_id=1, source_target_pairs={{0,4},{2,6},{4,0},{6,2},{8,12},{10,14},{12,8},{14,10},{16,20},{18,... | collective-permute-start | bytes 884744 | tf_op jit(solution)/shard_map/ppermute | solution.py:495
  216.7 22.1 %collective-permute-start.8 = (bf16[2,96,768]{2,1,0:T(8,128)(2,1)S(1)}, bf16[2,96,768]{2,1,0:T(8,128)(2,1)S(1)}, u32[]{:S(2)}, u32[]{:S(2)}) collective-permute-start(bf16[2,96,768]{2,1,0:T(8,128)(2,1)S(1)} %get-tuple-element.63), channel_id=1, source_target_pairs={{0,6},{2,0},{4,2},{6,4},{8,14},{10,8},{12,10},{14,12},{16,22},{18,... | collective-permute-start | bytes 884744 | tf_op jit(solution)/shard_map/ppermute | solution.py:495
  252.5 5.7 %collective-permute-start.10 = (bf16[208,384]{1,0:T(8,128)(2,1)S(1)}, bf16[208,384]{1,0:T(8,128)(2,1)S(1)}, u32[]{:S(2)}, u32[]{:S(2)}) collective-permute-start(bf16[208,384]{1,0:T(8,128)(2,1)S(1)} %reduce_sum.110), channel_id=1, source_target_pairs={{0,64},{1,65},{32,96},{33,97},{64,0},{65,1},{96,32},{97,33},{2,66}... | collective-permute-start | bytes 479240 | tf_op jit(solution)/shard_map/ppermute | solution.py:611
  253.3 6.8 %collective-permute-start.11 = (bf16[208,384]{1,0:T(8,128)(2,1)S(1)}, bf16[208,384]{1,0:T(8,128)(2,1)S(1)}, u32[]{:S(2)}, u32[]{:S(2)}) collective-permute-start(bf16[208,384]{1,0:T(8,128)(2,1)S(1)} %reduce_sum.110), channel_id=1, source_target_pairs={{0,65},{1,0},{32,97},{33,32},{64,1},{65,64},{96,33},{97,96},{2,67}... | collective-permute-start | bytes 479240 | tf_op jit(solution)/shard_map/ppermute | solution.py:611
  256.1 6.8 %collective-permute-start.9 = (bf16[208,384]{1,0:T(8,128)(2,1)S(1)}, bf16[208,384]{1,0:T(8,128)(2,1)S(1)}, u32[]{:S(2)}, u32[]{:S(2)}) collective-permute-start(bf16[208,384]{1,0:T(8,128)(2,1)S(1)} %reduce_sum.110), channel_id=1, source_target_pairs={{0,1},{1,64},{32,33},{33,96},{64,65},{65,0},{96,97},{97,32},{2,3},... | collective-permute-start | bytes 479240 | tf_op jit(solution)/shard_map/ppermute | solution.py:611
  263.7 68.8 %copy-start.13 = (bf16[128,384]{1,0:T(8,128)(2,1)S(1)}, bf16[128,384]{1,0:T(8,128)(2,1)}, u32[]{:S(2)}) copy-start(bf16[128,384]{1,0:T(8,128)(2,1)} %get-tuple-element.43) | copy-start | bytes 294916
  263.7 68.8 %copy-start.14 = (bf16[128,384]{1,0:T(8,128)(2,1)S(1)}, bf16[128,384]{1,0:T(8,128)(2,1)}, u32[]{:S(2)}) copy-start(bf16[128,384]{1,0:T(8,128)(2,1)} %get-tuple-element.42) | copy-start | bytes 294916
  263.7 68.8 %copy-start.8 = (f32[2,96,768]{2,1,0:T(8,128)S(1)}, f32[2,96,768]{2,1,0:T(8,128)}, u32[]{:S(2)}) copy-start(f32[2,96,768]{2,1,0:T(8,128)} %fusion.6.refs_0_) | copy-start | bytes 1769476
  263.7 69.7 %all-to-all-start.3 = ((bf16[16,768,128]{2,1,0:T(8,128)(2,1)}), bf16[16,768,128]{2,1,0:T(8,128)(2,1)}, u32[]{:S(2)}, u32[]{:S(2)}) async-start(bf16[16,768,128]{2,1,0:T(8,128)(2,1)} %spread.1), calls=%async_computation.3 | async-start | bytes 6291456 | tf_op jit(solution)/shard_map/all_to_all | solution.py:623
  331.2 6.5 %collective-permute-start.12 = (bf16[16,208,384]{2,1,0:T(8,128)(2,1)}, bf16[16,208,384]{2,1,0:T(8,128)(2,1)}, u32[]{:S(2)}, u32[]{:S(2)}) collective-permute-start(bf16[16,208,384]{2,1,0:T(8,128)(2,1)} %bitcast.79), channel_id=1, source_target_pairs={{0,32},{32,0},{64,96},{96,64},{1,33},{33,1},{65,97},{97,65},{2,34}... | collective-permute-start | bytes 7667720 | tf_op jit(solution)/shard_map/ppermute | solution.py:613
  333.4 2.6 copy-start.3
  335.9 0.8 copy-start.26
  335.9 0.9 copy-start.24
  340.5 7.0 %copy-start.1 = (bf16[768,768]{1,0:T(8,128)(2,1)S(1)}, bf16[768,768]{1,0:T(8,128)(2,1)}, u32[]{:S(2)}) copy-start(bf16[768,768]{1,0:T(8,128)(2,1)} %param.20) | copy-start | bytes 3538948
Sparse Core Ops, SparseCore 0:
  10.9 50.7 all-gather.3
  263.8 67.3 all-gather.5

commit v3 on v2

--- a/solution.py
+++ b/solution.py
@@ -593,12 +593,12 @@
     expert_sum = paired[0].astype(F32)
     for step in range(1, side):
         expert_sum = expert_sum + ring(paired[step], False, step).astype(F32)
+    part = spread(core, w_key, w_value, terms_b, terms_a, tok_count, (merged,))
+    merged = lax.all_to_all(merged, "context", split_axis=0, concat_axis=0, tiled=True)
+    merged = jnp.sum(merged.astype(F32), axis=0).astype(BF16)
+    part, merged, expert_sum = lax.optimization_barrier((part, merged, expert_sum))
     grad_w_in_out = expert_sum[0].T[None]
     grad_w_out_out = expert_sum[1][None]
-    part = spread(core, w_key, w_value, terms_b, terms_a, tok_count, (expert_sum, merged))
-    merged = lax.all_to_all(merged, "context", split_axis=0, concat_axis=0, tiled=True)
-    merged = jnp.sum(merged.astype(F32), axis=0).astype(BF16)
-    part, merged = lax.optimization_barrier((part, merged))
     total = merged.astype(F32)
     depth = expert_count // 2 * dp_count
     for step in range(1, depth):

time: 355 us -> 344 us (0.969)
  waiting for transfers between devices: 156 us -> 145 us
    ppermute x6, waiting for transfers between devices: 21.3 us -> 10.8 us  [ring(): return lax.ppermute(values, 'context', pairs)]
    unnamed x57 -> x55, local copies, waits for them, and re-layouts: 7.27 us -> 7.26 us
  transfers between devices with their start and end apart: 18 -> 18, of which waited for: 9 -> 9; matrix products, arithmetic and copies ran while one was open for 8% -> 8% of each run, Pallas kernels for 14% -> 15%
where the time goes in v3:
time: 344 us; the launch traced here: 343 us
  waiting for transfers between devices  145 us (42%)
  Pallas kernels  99.8 us (29%)
  starting transfers between devices  28 us (8%)
  local copies, waits for them, and re-layouts  17.8 us (5%)
  other arithmetic  16.1 us (5%)
  between operations  14.6 us (4%)
  blocking collectives  14.3 us (4%)
  matrix products  7.13 us (2%)
    all_gather x1, waiting for transfers between devices, per_device(): whole = lax.all_gather(total.astype(BF16), 'context', axis=0)  62.8 us
    all_gather x1, waiting for transfers between devices, per_device(): act_all = lax.all_gather(act, 'context', axis=0, tiled=True)  37.9 us
    pallas_call x2, Pallas kernels, attend_back(): pl.pallas_call(attend_back_kernel, grid_spec=pltpu.PrefetchScalarGridSpec...  31.8 us
    pallas_call x1, Pallas kernels, attend(): pl.pallas_call(attend_kernel, grid=(pairs,), in_specs=[whole(length), who...  28.6 us
    ppermute x1, waiting for transfers between devices, per_device(): other = lax.ppermute(shares[1], 'dp', [(0, 1), (1, 0)])  22.3 us
    all_to_all x1, blocking collectives, per_device(): lax.all_to_all(going, 'expert', split_axis=0, concat_axis=0, tiled=True)  14.3 us
    ppermute x6, waiting for transfers between devices, ring(): return lax.ppermute(values, 'context', pairs)  10.8 us
    pallas_call x1, Pallas kernels, spread(): pl.pallas_call(spread_kernel, grid_spec=pltpu.PrefetchScalarGridSpec(num_...  10.6 us
  transfers between devices with their start and end apart: 18, of which 9 were waited for; matrix products, arithmetic and copies ran while one was open for 8% of the time, Pallas kernels for 15%

profile of v3, /device:TPU:1, one launch (start us, length us, event | category | flops | bytes accessed | tf_op | source)
XLA Modules:
  0.0 343.0 jit_solution(3613197174348722201)
XLA Ops:
  7.2 1.1 fusion.9
  8.4 0.7 convert_element_type.132
  9.1 1.7 fusion.11.own_ref
  10.8 1.4 constant_dynamic-slice_fusion
  12.2 1.5 copy.38
  13.9 0.7 reshape.142.win_ref
  14.6 2.4 copy.39
  17.1 1.5 copy.40
  18.6 2.4 copy.41
  21.4 2.4 dynamic-slice_bitcast_fusion.refs_1_.refs_5_
  23.8 37.9 %all-gather.4.cloned.1.call-done.act_ref = bf16[2048,768]{1,0:T(8,128)(2,1)} async-done(((bf16[128,768]{1,0:T(8,128)(2,1)}), bf16[2048,768]{1,0:T(8,128)(2,1)}) %all-gather.4.cloned.1.call-update) | async-done | bytes 3145744 | tf_op jit(solution)/shard_map/all_gather | solution.py:501
  61.7 28.6 %attend.1 = (bf16[128,768]{1,0:T(8,128)(2,1)}, bf16[2048,768]{1,0:T(8,128)(2,1)}, bf16[2048,768]{1,0:T(8,128)(2,1)}, f32[128,768]{1,0:T(8,128)}, f32[128,768]{1,0:T(8,128)}, /*index=5*/bf16[6,256,2048]{2,1,0:T(8,128)(2,1)}) custom-call(bf16[2048,768]{1,0:T(8,128)(2,1)} %all-gather.4.cloned.1.call-done.act_ref, bf16[128,768]{1,0:T(8,128)(2,1)} %fusion.11.own_ref, ...), custom_call_target="tpu_custom_call" | custom-call | flops 6442450944 | bytes 25165824 | tf_op jit(solution)/shard_map/attend/pallas_call | solution.py:120
  90.4 1.5 multiply_reduce_fusion.2
  92.8 14.3 %all_to_all.20 = bf16[4,40,1536]{2,1,0:T(8,128)(2,1)} all-to-all(bf16[4,40,1536]{2,1,0:T(8,128)(2,1)S(1)} %bitcast.83), channel_id=1, replica_groups=mesh['expert'=4,'context'=16,'dp'=2] {'expert'}, dimensions={0} | all-to-all | bytes 983040 | tf_op jit(solution)/shard_map/all_to_all | solution.py:541
  107.1 9.0 %expert_both.1 = bf16[160,1536]{1,0:T(8,128)(2,1)} custom-call(bf16[160,1536]{1,0:T(8,128)(2,1)} %bitcast.95, bf16[768,3072]{1,0:T(8,128)(2,1)} %bitcast.102, bf16[3072,768]{1,0:T(8,128)(2,1)} %bitcast.103), custom_call_target="tpu_custom_call" | custom-call | flops 3019898880 | bytes 9437184 | tf_op jit(solution)/shard_map/expert_both/pallas_call | solution.py:393
  116.1 4.4 %all-to-all-start.1 = ((bf16[4,40,1536]{2,1,0:T(8,128)(2,1)}), bf16[4,40,1536]{2,1,0:T(8,128)(2,1)S(1)}, u32[]{:S(2)}, u32[]{:S(2)}) async-start(bf16[4,40,1536]{2,1,0:T(8,128)(2,1)} %bitcast.101), calls=%async_computation.1 | async-start | bytes 983040 | tf_op jit(solution)/shard_map/all_to_all | solution.py:545
  120.5 0.6 pad_add_fusion.place_ref
  121.1 0.4 collective-permute-start
  121.5 2.4 collective-permute-start.1
  123.9 0.8 collective-permute-start.2
  124.7 4.9 %all-to-all-done.1 = bf16[4,40,1536]{2,1,0:T(8,128)(2,1)S(1)} async-done(((bf16[4,40,1536]{2,1,0:T(8,128)(2,1)}), bf16[4,40,1536]{2,1,0:T(8,128)(2,1)S(1)}, u32[]{:S(2)}, u32[]{:S(2)}) %all-to-all-start.1) | async-done | bytes 491552 | tf_op jit(solution)/shard_map/all_to_all | solution.py:545
  129.9 0.8 fusion.8
  130.8 0.5 multiply_reduce_fusion
  131.9 1.2 fusion.4.do_ref
  133.5 1.1 collective-permute-start.4
  134.6 15.9 %attend_back.3 = (bf16[128,384]{1,0:T(8,128)(2,1)}, bf16[2,384,2048]{2,1,0:T(8,128)(2,1)}, bf16[3,768,384]{2,1,0:T(8,128)(2,1)}, f32[1,768]{1,0:T(1,128)}, f32[3,2,2176]{2,1,0:T(2,128)}) custom-call(s32[1]{0:T(128)S(6)} %sub.41.half_ref, bf16[6,256,2048]{2,1,0:T(8,128)(2,1)} %get-tuple-element.38.p_ref, bf16[128,768]{1,0:T(8,128)(2,1)} %fusion.4.do_ref, ...), custom_call_target="tpu_custom_call" | custom-call | flops 6442450944 | bytes 14155776 | tf_op jit(solution)/shard_map/attend_back/pallas_call | solution.py:221
  150.6 1.2 convolution_convert_fusion.2.mine_out_ref
  151.8 8.8 %expert_grads.1.ready_ref = bf16[2,4,2,96,768]{4,3,2,1,0:T(8,128)(2,1)} custom-call(s32[2]{0:T(128)} %pad_add_fusion.place_ref, bf16[160,1536]{1,0:T(8,128)(2,1)} %bitcast.97, bf16[160,1536]{1,0:T(8,128)(2,1)} %collective-permute-done.refs_1_, bf16[160,1536]{1,0:T(8,128)(2,1)} %collective-permute-done.1.refs_2_, ...), custom_call_target="tpu_custom_call" | custom-call | flops 3019898880 | bytes 4718592 | tf_op jit(solution)/shard_map/expert_grads/pallas_call | solution.py:439
  160.6 15.9 %attend_back.2 = (bf16[128,384]{1,0:T(8,128)(2,1)}, bf16[2,384,2048]{2,1,0:T(8,128)(2,1)}, bf16[3,768,384]{2,1,0:T(8,128)(2,1)}, f32[1,768]{1,0:T(1,128)}, f32[3,2,2176]{2,1,0:T(2,128)}) custom-call(s32[1]{0:T(128)} %bitcast.18.half_ref.core_ref, bf16[6,256,2048]{2,1,0:T(8,128)(2,1)} %get-tuple-element.38.p_ref, bf16[128,768]{1,0:T(8,128)(2,1)} %fusion.4.do_ref, ...), custom_call_target="tpu_custom_call" | custom-call | flops 6442450944 | bytes 14155776 | tf_op jit(solution)/shard_map/attend_back/pallas_call | solution.py:221
  176.5 0.8 broadcast_select_fusion.3
  177.8 0.7 add_reduce_fusion
  178.6 0.8 reshape.150.small_ref
  179.4 0.8 copy-done.9
  180.2 4.7 %merge_halves.1.refs_0_ = bf16[16,208,384]{2,1,0:T(8,128)(2,1)} custom-call(bf16[3,768,384]{2,1,0:T(8,128)(2,1)} %get-tuple-element.47.mine_ref, bf16[3,768,384]{2,1,0:T(8,128)(2,1)} %collective-permute-done.3.other_ref, bf16[768,384]{1,0:T(8,128)(2,1)} %convolution_convert_fusion.2.mine_out_ref, bf16[768,384]{1,0:T(8,128)(2,1)} %copy-done.9, ...), custom_call_target="tpu_custom_call" | custom-call | tf_op jit(solution)/shard_map/merge_halves/pallas_call | solution.py:318
  185.0 0.4 collective-permute-start.5
  185.4 4.5 %all-to-all-start.2 = ((bf16[16,208,384]{2,1,0:T(8,128)(2,1)}), bf16[16,208,384]{2,1,0:T(8,128)(2,1)}, u32[]{:S(2)}, u32[]{:S(2)}) async-start(bf16[16,208,384]{2,1,0:T(8,128)(2,1)} %merge_halves.1.refs_0_), calls=%async_computation.2 | async-start | bytes 5111808 | tf_op jit(solution)/shard_map/all_to_all | solution.py:597
  189.9 22.3 %collective-permute-done.5 = bf16[4,2,96,768]{3,2,1,0:T(8,128)(2,1)S(1)} collective-permute-done((bf16[4,2,96,768]{3,2,1,0:T(8,128)(2,1)S(1)}, bf16[4,2,96,768]{3,2,1,0:T(8,128)(2,1)S(1)}, u32[]{:S(2)}, u32[]{:S(2)}) %collective-permute-start.5) | collective-permute-done | bytes 1179680 | tf_op jit(solution)/shard_map/ppermute | solution.py:591
  212.2 1.5 fusion
  213.8 0.5 collective-permute-start.6
  214.4 2.4 collective-permute-start.7
  216.7 0.8 collective-permute-start.8
  217.6 10.6 %spread.1 = bf16[16,768,128]{2,1,0:T(8,128)(2,1)} custom-call(s32[1]{0:T(128)} %bitcast.18.half_ref.core_ref, bf16[768,768]{1,0:T(8,128)(2,1)} %wkb_ref.1, bf16[768,768]{1,0:T(8,128)(2,1)} %wvb_ref.1, bf16[2,384,2048]{2,1,0:T(8,128)(2,1)} %get-tuple-element.45.a_ref, bf16[768,768]{1,0:T(8,128)(2,1)} %wkb_ref.1, bf16[768,768]{1,0:T(8,128)(2,1)} %wvb_ref.1, ...), custom_call_target="tpu_custom_call" | custom-call | flops 4831838208 | bytes 9437184 | tf_op jit(solution)/shard_map/spread/pallas_call | solution.py:279
  228.1 2.6 collective-permute-done.6
  230.7 8.2 %collective-permute-done.7 = bf16[2,96,768]{2,1,0:T(8,128)(2,1)S(1)} collective-permute-done((bf16[2,96,768]{2,1,0:T(8,128)(2,1)S(1)}, bf16[2,96,768]{2,1,0:T(8,128)(2,1)S(1)}, u32[]{:S(2)}, u32[]{:S(2)}) %collective-permute-start.7) | collective-permute-done | bytes 294944 | tf_op jit(solution)/shard_map/ppermute | solution.py:495
  239.1 2.1 reduce_sum.110
  241.2 0.8 collective-permute-start.10
  242.0 2.9 collective-permute-start.11
  244.9 2.0 collective-permute-done.10
  246.9 1.9 collective-permute-done.11
  248.8 2.5 collective-permute-done.9
  251.4 0.8 add_convert_fusion.1
  252.2 5.0 %all-to-all-start.3 = ((bf16[16,768,128]{2,1,0:T(8,128)(2,1)}), bf16[16,768,128]{2,1,0:T(8,128)(2,1)}, u32[]{:S(2)}, u32[]{:S(2)}) async-start(bf16[16,768,128]{2,1,0:T(8,128)(2,1)} %spread.1), calls=%async_computation.3 | async-start | bytes 6291456 | tf_op jit(solution)/shard_map/all_to_all | solution.py:623
  257.2 62.8 %all-gather.6.cloned.1.call-done = bf16[3328,384]{1,0:T(8,128)(2,1)} async-done(((bf16[208,384]{1,0:T(8,128)(2,1)}), bf16[3328,384]{1,0:T(8,128)(2,1)}) %all-gather.6.cloned.1.call-update) | async-done | bytes 2555920 | tf_op jit(solution)/shard_map/all_gather | solution.py:612
  319.9 1.4 collective-permute-start.12
  321.3 0.8 fusion.63
  322.2 2.4 convert_reduce_fusion
  324.8 0.6 fusion.12
  325.5 0.9 fusion.29
  326.4 1.1 convert_add_fusion.3
  327.5 0.4 split.17
  328.0 0.6 slice_bitcast_fusion.7
  328.6 0.6 slice_bitcast_fusion.6
  329.2 0.6 fusion.64
  329.8 6.4 %unpack_halves.1 = (f32[768,768]{1,0:T(8,128)}, f32[768,768]{1,0:T(8,128)}, f32[768,768]{1,0:T(8,128)}, f32[768,768]{1,0:T(8,128)}) custom-call(s32[1]{0:T(128)} %bitcast.18.half_ref.core_ref, bf16[16,208,384]{2,1,0:T(8,128)(2,1)} %bitcast.81, bf16[16,208,384]{2,1,0:T(8,128)(2,1)} %collective-permute-done.12.other_ref), custom_call_target="tpu_custom_call" | custom-call | tf_op jit(solution)/shard_map/unpack_halves/pallas_call | solution.py:350
  (103 shorter events, 4.2 us)
Async XLA Ops:
  7.2 83.2 %copy-start = (bf16[768,768]{1,0:T(8,128)(2,1)S(1)}, bf16[768,768]{1,0:T(8,128)(2,1)}, u32[]{:S(2)}) copy-start(bf16[768,768]{1,0:T(8,128)(2,1)} %param.20) | copy-start | bytes 3538948
  7.2 54.5 %all-gather.4.cloned.1.call-start = ((), (), s32[]{:S(2)}) async-start(), calls=%async_computation.4 | async-start | bytes 3342336 | tf_op jit(solution)/shard_map/all_gather | solution.py:501
  8.4 5.3 %copy-start.24 = (f32[128]{0:T(128)}, f32[128]{0:T(128)S(1)}, u32[]{:S(2)}) copy-start(f32[128]{0:T(128)S(1)} %fusion.9) | copy-start | bytes 1540
  12.2 1.5 copy-start.16
  12.2 1.6 copy-start.19
  13.7 3.4 copy-start.8
  18.6 2.4 copy-start.21
  18.6 2.4 copy-start.17
  61.7 28.7 %copy-start.2 = (bf16[1,128,768]{2,1,0:T(8,128)(2,1)S(1)}, bf16[1,128,768]{2,1,0:T(8,128)(2,1)}, u32[]{:S(2)}) copy-start(bf16[1,128,768]{2,1,0:T(8,128)(2,1)} %param.14) | copy-start | bytes 589828
  90.3 1.5 copy-start.15
  90.3 2.0 copy-start.6
  107.1 14.0 %copy-start.10 = (bf16[4,40,1536]{2,1,0:T(8,128)(2,1)S(1)}, bf16[4,40,1536]{2,1,0:T(8,128)(2,1)}, u32[]{:S(2)}) copy-start(bf16[4,40,1536]{2,1,0:T(8,128)(2,1)} %all_to_all.20) | copy-start | bytes 1474564
  116.1 13.5 %all-to-all-start.1 = ((bf16[4,40,1536]{2,1,0:T(8,128)(2,1)}), bf16[4,40,1536]{2,1,0:T(8,128)(2,1)S(1)}, u32[]{:S(2)}, u32[]{:S(2)}) async-start(bf16[4,40,1536]{2,1,0:T(8,128)(2,1)} %bitcast.101), calls=%async_computation.1 | async-start | bytes 983040 | tf_op jit(solution)/shard_map/all_to_all | solution.py:545
  121.1 30.7 %collective-permute-start = (bf16[160,1536]{1,0:T(8,128)(2,1)S(1)}, bf16[160,1536]{1,0:T(8,128)(2,1)}, u32[]{:S(2)}, u32[]{:S(2)}) collective-permute-start(bf16[160,1536]{1,0:T(8,128)(2,1)S(1)} %bitcast.98), channel_id=1, source_target_pairs={{0,8},{2,10},{4,12},{6,14},{8,16},{10,18},{12,20},{14,22},{16,24},... | collective-permute-start | bytes 1474568 | tf_op jit(solution)/shard_map/ppermute | solution.py:495
  121.5 30.3 %collective-permute-start.1 = (bf16[160,1536]{1,0:T(8,128)(2,1)S(1)}, bf16[160,1536]{1,0:T(8,128)(2,1)}, u32[]{:S(2)}, u32[]{:S(2)}) collective-permute-start(bf16[160,1536]{1,0:T(8,128)(2,1)S(1)} %bitcast.99), channel_id=1, source_target_pairs={{0,16},{2,18},{4,20},{6,22},{8,24},{10,26},{12,28},{14,30},{16,0},... | collective-permute-start | bytes 1474568 | tf_op jit(solution)/shard_map/ppermute | solution.py:495
  123.9 27.9 %collective-permute-start.2 = (bf16[160,1536]{1,0:T(8,128)(2,1)S(1)}, bf16[160,1536]{1,0:T(8,128)(2,1)}, u32[]{:S(2)}, u32[]{:S(2)}) collective-permute-start(bf16[160,1536]{1,0:T(8,128)(2,1)S(1)} %bitcast.100), channel_id=1, source_target_pairs={{0,24},{2,26},{4,28},{6,30},{8,0},{10,2},{12,4},{14,6},{16,8},{18,... | collective-permute-start | bytes 1474568 | tf_op jit(solution)/shard_map/ppermute | solution.py:495
  130.7 1.1 copy-start.11
  131.7 1.4 copy-start.22
  131.7 1.4 copy-start.4
  133.5 45.9 %collective-permute-start.4 = (bf16[768,384]{1,0:T(8,128)(2,1)S(1)}, bf16[768,384]{1,0:T(8,128)(2,1)S(1)}, u32[]{:S(2)}, u32[]{:S(2)}) collective-permute-start(bf16[768,384]{1,0:T(8,128)(2,1)S(1)} %convolution_convert_fusion.1), channel_id=1, source_target_pairs={{0,32},{32,0},{64,96},{96,64},{1,33},{33,1},{65,97},{97,65},{2,34}... | collective-permute-start | bytes 1769480 | tf_op jit(solution)/shard_map/ppermute | solution.py:570
  134.6 16.0 %copy-start.5 = (f32[128,768]{1,0:T(8,128)S(1)}, f32[128,768]{1,0:T(8,128)}, u32[]{:S(2)}) copy-start(f32[128,768]{1,0:T(8,128)} %get-tuple-element.37.o_ref) | copy-start | bytes 1179652
  150.5 28.9 %collective-permute-start.3 = (bf16[3,768,384]{2,1,0:T(8,128)(2,1)}, bf16[3,768,384]{2,1,0:T(8,128)(2,1)}, u32[]{:S(2)}, u32[]{:S(2)}) collective-permute-start(bf16[3,768,384]{2,1,0:T(8,128)(2,1)} %get-tuple-element.48), channel_id=1, source_target_pairs={{0,32},{32,0},{64,96},{96,64},{1,33},{33,1},{65,97},{97,65},{2,34}... | collective-permute-start | bytes 5308424 | tf_op jit(solution)/shard_map/ppermute | solution.py:576
  160.6 15.9 %copy-start.14 = (f32[3,2,2176]{2,1,0:T(2,128)S(1)}, f32[3,2,2176]{2,1,0:T(2,128)}, u32[]{:S(2)}) copy-start(f32[3,2,2176]{2,1,0:T(2,128)} %get-tuple-element.52) | copy-start | bytes 156676
  160.6 17.3 %copy-start.20 = (f32[1,768]{1,0:T(1,128)S(1)}, f32[1,768]{1,0:T(1,128)}, u32[]{:S(2)}) copy-start(f32[1,768]{1,0:T(1,128)} %get-tuple-element.49) | copy-start | bytes 9220
  160.6 18.0 %copy-start.18 = (bf16[768]{0:T(1024)(128)(2,1)S(1)}, bf16[768]{0:T(1024)(128)(2,1)}, u32[]{:S(2)}) copy-start(bf16[768]{0:T(1024)(128)(2,1)} %param.16) | copy-start | bytes 4612
  179.4 0.8 copy-start.9
  180.2 4.7 %copy-start.7 = (bf16[2,4,2,96,768]{4,3,2,1,0:T(8,128)(2,1)S(1)}, bf16[2,4,2,96,768]{4,3,2,1,0:T(8,128)(2,1)}, u32[]{:S(2)}) copy-start(bf16[2,4,2,96,768]{4,3,2,1,0:T(8,128)(2,1)} %expert_grads.1.ready_ref) | copy-start | bytes 7077892
  185.0 27.3 %collective-permute-start.5 = (bf16[4,2,96,768]{3,2,1,0:T(8,128)(2,1)S(1)}, bf16[4,2,96,768]{3,2,1,0:T(8,128)(2,1)S(1)}, u32[]{:S(2)}, u32[]{:S(2)}) collective-permute-start(bf16[4,2,96,768]{3,2,1,0:T(8,128)(2,1)S(1)} %slice_bitcast_fusion), channel_id=1, source_target_pairs={{0,1},{1,0},{2,3},{3,2},{4,5},{5,4},{6,7},{7,6},{8,9},{9,8},{10,11... | collective-permute-start | bytes 3538952 | tf_op jit(solution)/shard_map/ppermute | solution.py:591
  185.4 53.7 %all-to-all-start.2 = ((bf16[16,208,384]{2,1,0:T(8,128)(2,1)}), bf16[16,208,384]{2,1,0:T(8,128)(2,1)}, u32[]{:S(2)}, u32[]{:S(2)}) async-start(bf16[16,208,384]{2,1,0:T(8,128)(2,1)} %merge_halves.1.refs_0_), calls=%async_computation.2 | async-start | bytes 5111808 | tf_op jit(solution)/shard_map/all_to_all | solution.py:597
  189.9 130.0 %all-gather.6.cloned.1.call-start = ((), (), s32[]{:S(2)}) async-start(), calls=%async_computation.5 | async-start | bytes 2715648 | tf_op jit(solution)/shard_map/all_gather | solution.py:612
  213.8 16.9 %collective-permute-start.6 = (bf16[2,96,768]{2,1,0:T(8,128)(2,1)S(1)}, bf16[2,96,768]{2,1,0:T(8,128)(2,1)S(1)}, u32[]{:S(2)}, u32[]{:S(2)}) collective-permute-start(bf16[2,96,768]{2,1,0:T(8,128)(2,1)S(1)} %get-tuple-element.64), channel_id=1, source_target_pairs={{0,2},{2,4},{4,6},{6,0},{8,10},{10,12},{12,14},{14,8},{16,18},{18,... | collective-permute-start | bytes 884744 | tf_op jit(solution)/shard_map/ppermute | solution.py:495
  214.4 24.6 %collective-permute-start.7 = (bf16[2,96,768]{2,1,0:T(8,128)(2,1)S(1)}, bf16[2,96,768]{2,1,0:T(8,128)(2,1)S(1)}, u32[]{:S(2)}, u32[]{:S(2)}) collective-permute-start(bf16[2,96,768]{2,1,0:T(8,128)(2,1)S(1)} %get-tuple-element.66), channel_id=1, source_target_pairs={{0,4},{2,6},{4,0},{6,2},{8,12},{10,14},{12,8},{14,10},{16,20},{18,... | collective-permute-start | bytes 884744 | tf_op jit(solution)/shard_map/ppermute | solution.py:495
  216.7 22.2 %collective-permute-start.8 = (bf16[2,96,768]{2,1,0:T(8,128)(2,1)S(1)}, bf16[2,96,768]{2,1,0:T(8,128)(2,1)S(1)}, u32[]{:S(2)}, u32[]{:S(2)}) collective-permute-start(bf16[2,96,768]{2,1,0:T(8,128)(2,1)S(1)} %get-tuple-element.65), channel_id=1, source_target_pairs={{0,6},{2,0},{4,2},{6,4},{8,14},{10,8},{12,10},{14,12},{16,22},{18,... | collective-permute-start | bytes 884744 | tf_op jit(solution)/shard_map/ppermute | solution.py:495
  241.2 5.7 %collective-permute-start.10 = (bf16[208,384]{1,0:T(8,128)(2,1)S(1)}, bf16[208,384]{1,0:T(8,128)(2,1)S(1)}, u32[]{:S(2)}, u32[]{:S(2)}) collective-permute-start(bf16[208,384]{1,0:T(8,128)(2,1)S(1)} %reduce_sum.110), channel_id=1, source_target_pairs={{0,64},{1,65},{32,96},{33,97},{64,0},{65,1},{96,32},{97,33},{2,66}... | collective-permute-start | bytes 479240 | tf_op jit(solution)/shard_map/ppermute | solution.py:611
  242.0 6.9 %collective-permute-start.11 = (bf16[208,384]{1,0:T(8,128)(2,1)S(1)}, bf16[208,384]{1,0:T(8,128)(2,1)S(1)}, u32[]{:S(2)}, u32[]{:S(2)}) collective-permute-start(bf16[208,384]{1,0:T(8,128)(2,1)S(1)} %reduce_sum.110), channel_id=1, source_target_pairs={{0,65},{1,0},{32,97},{33,32},{64,1},{65,64},{96,33},{97,96},{2,67}... | collective-permute-start | bytes 479240 | tf_op jit(solution)/shard_map/ppermute | solution.py:611
  244.9 6.5 %collective-permute-start.9 = (bf16[208,384]{1,0:T(8,128)(2,1)S(1)}, bf16[208,384]{1,0:T(8,128)(2,1)S(1)}, u32[]{:S(2)}, u32[]{:S(2)}) collective-permute-start(bf16[208,384]{1,0:T(8,128)(2,1)S(1)} %reduce_sum.110), channel_id=1, source_target_pairs={{0,1},{1,64},{32,33},{33,96},{64,65},{65,0},{96,97},{97,32},{2,3},... | collective-permute-start | bytes 479240 | tf_op jit(solution)/shard_map/ppermute | solution.py:611
  252.1 69.1 %copy-start.12 = (bf16[128,384]{1,0:T(8,128)(2,1)S(1)}, bf16[128,384]{1,0:T(8,128)(2,1)}, u32[]{:S(2)}) copy-start(bf16[128,384]{1,0:T(8,128)(2,1)} %get-tuple-element.44) | copy-start | bytes 294916
  252.2 69.1 %copy-start.13 = (bf16[128,384]{1,0:T(8,128)(2,1)S(1)}, bf16[128,384]{1,0:T(8,128)(2,1)}, u32[]{:S(2)}) copy-start(bf16[128,384]{1,0:T(8,128)(2,1)} %get-tuple-element.43) | copy-start | bytes 294916
  252.2 70.0 %all-to-all-start.3 = ((bf16[16,768,128]{2,1,0:T(8,128)(2,1)}), bf16[16,768,128]{2,1,0:T(8,128)(2,1)}, u32[]{:S(2)}, u32[]{:S(2)}) async-start(bf16[16,768,128]{2,1,0:T(8,128)(2,1)} %spread.1), calls=%async_computation.3 | async-start | bytes 6291456 | tf_op jit(solution)/shard_map/all_to_all | solution.py:623
  319.9 6.5 %collective-permute-start.12 = (bf16[16,208,384]{2,1,0:T(8,128)(2,1)}, bf16[16,208,384]{2,1,0:T(8,128)(2,1)}, u32[]{:S(2)}, u32[]{:S(2)}) collective-permute-start(bf16[16,208,384]{2,1,0:T(8,128)(2,1)} %bitcast.79), channel_id=1, source_target_pairs={{0,32},{32,0},{64,96},{96,64},{1,33},{33,1},{65,97},{97,65},{2,34}... | collective-permute-start | bytes 7667720 | tf_op jit(solution)/shard_map/ppermute | solution.py:613
  322.2 2.6 copy-start.3
  324.6 0.8 copy-start.25
  324.6 0.9 copy-start.23
  329.2 7.0 %copy-start.1 = (bf16[768,768]{1,0:T(8,128)(2,1)S(1)}, bf16[768,768]{1,0:T(8,128)(2,1)}, u32[]{:S(2)}) copy-start(bf16[768,768]{1,0:T(8,128)(2,1)} %param.20) | copy-start | bytes 3538948
Sparse Core Ops, SparseCore 0:
  10.9 50.7 all-gather.3
  252.3 67.6 all-gather.5
